TPU v7x, 512 devices: a whole 4x8x8 slice. The times are simulated.
512 devices in a mesh: chan: 32 (over z_lo, y, core), spec: 16 (over z_hi, x).
Axes of the slice: x: 4, y: 8, z: 8 (z_hi: 4, z_lo: 2; z = z_hi * 2 + z_lo), core: 2. Of those that a mesh axis runs over, the one named last changes fastest.
Arguments:
- record: bfloat16 [4096, 32, 1152], P('chan', 'spec'), may hold values from -6 to 6
- offsets: int32 [32], P('spec'), may hold values from 0 to 128
- sources: int32 [16], replicated, may hold values from 0 to 4095
Outputs:
- lagged: bfloat16 [512, 16, 4096], P('spec', None, 'chan')
All inputs are finite; a program needn't handle non-finite values.
Results may differ from a plain program's by a relative error of at most 0.017.
Values may be sent and summed in bfloat16 or wider, within the bound.
A program may use at most 64 MiB of HBM per device.

v0:
```python
import functools
import math

import jax
import jax.numpy as jnp
import numpy as np
from jax import lax
from jax.experimental import pallas as pl
from jax.experimental.pallas import tpu as pltpu
from jax.sharding import PartitionSpec as P

SAMPLES = 1024
HALF = SAMPLES // 2
PAD = 128
NSRC = 16
WATER = 0.1
NX = 4
ROWS = 128
WIN = 2
BLK = ROWS // NX
GROUPS = 32
PIECES = 32
F32 = jnp.float32
BF16 = jnp.bfloat16
MESH = pl.DeviceIdType.MESH


def forward_tables():
    rows = np.arange(SAMPLES)[:, None]
    cols = np.arange(SAMPLES)[None, :]
    freq = rows % HALF
    angle = 2.0 * np.pi / SAMPLES * (freq * cols % SAMPLES)
    alternating = 1.0 - 2.0 * (cols % 2)
    imag = np.where(freq == 0, alternating, -np.sin(angle))
    table = np.where(rows < HALF, np.cos(angle), imag)
    upper = table.astype(jnp.bfloat16)
    lower = (table - upper.astype(np.float64)).astype(jnp.bfloat16)
    return upper, lower


def inverse_table(windows):
    shifted = np.arange(HALF)[:, None] - HALF // 2
    freq = (np.arange(16)[:, None] + 16 * np.arange(GROUPS)[None, :]).reshape(1, -1)
    angle = 2.0 * np.pi / SAMPLES * (freq * shifted % SAMPLES)
    alternating = 1.0 - 2.0 * (shifted % 2)
    first = freq == 0
    real = np.where(first, 1.0, 2.0 * np.cos(angle))
    imag = np.where(first, alternating, -2.0 * np.sin(angle))
    table = np.concatenate([real, imag], axis=1) / math.sqrt(windows * SAMPLES)
    return table.astype(jnp.bfloat16)


def spread_table():
    table = np.zeros((4, BLK, 4, 4, BLK))
    for quarter in range(4):
        for copy in range(4):
            table[quarter, np.arange(BLK), quarter, copy, np.arange(BLK)] = 1.0
    return table.reshape(128, 512).astype(jnp.bfloat16)


def diagonal_mask():
    mask = np.zeros((16, 16, BLK))
    mask[np.arange(16), np.arange(16)] = 1.0
    return mask.reshape(16, 512).astype(jnp.bfloat16)


def dot_t(left, right):
    return lax.dot_general(left, right, (((1,), (1,)), ((), ())), preferred_element_type=F32)


def dot(left, right):
    return lax.dot_general(left, right, (((1,), (0,)), ((), ())), preferred_element_type=F32)


def block_transpose(parts):
    count = len(parts)
    lane = lax.broadcasted_iota(jnp.int32, parts[0].shape, 1)
    step = count // 2
    while step:
        width = step * 128 // count
        low = (lane // width) % 2 == 0
        done = list(parts)
        for i in range(count):
            if (i // step) % 2 == 0:
                a, b = parts[i], parts[i + step]
                done[i] = jnp.where(low, a, pltpu.roll(b, width, 1))
                done[i + step] = jnp.where(low, pltpu.roll(a, 128 - width, 1), b)
        parts = done
        step //= 2
    return parts


def kernel(
    nchan,
    nz,
    offsets,
    sources,
    record,
    upper,
    lower,
    inverse,
    spread,
    mask,
    out,
    traces,
    pieces,
    reduced,
    gathered_x,
    piece_out,
    picked,
    spectrum,
    outgoing,
    incoming,
    left,
    copies,
    cross,
    stacked,
    lags_out,
    lags_in,
    finished,
    last,
    reduce_send,
    reduce_recv,
    x_send,
    x_recv,
    chan_send,
    chan_recv,
    white_send,
    white_recv,
    z_send,
    z_recv,
    last_send,
    last_recv,
):
    chan = lax.axis_index("chan")
    spec = lax.axis_index("spec")
    me_x = lax.rem(spec, NX)
    me_z = spec // NX
    per = PIECES // nchan
    lag_rows = HALF // nz

    def at_x(other):
        return (chan, me_z * NX + other)

    def at_z(other):
        return (chan, other * NX + me_x)

    barrier = pltpu.get_barrier_semaphore()

    @pl.loop(1, nchan)
    def _(step):
        pl.semaphore_signal(
            barrier, inc=1, device_id=(lax.rem(chan + step, nchan), spec), device_id_type=MESH
        )

    @pl.loop(1, NX)
    def _(step):
        pl.semaphore_signal(
            barrier, inc=1, device_id=at_x(lax.rem(me_x + step, NX)), device_id_type=MESH
        )

    @pl.loop(1, nz)
    def _(step):
        pl.semaphore_signal(
            barrier, inc=1, device_id=at_z(lax.rem(me_z + step, nz)), device_id_type=MESH
        )

    lane = lax.broadcasted_iota(jnp.int32, (ROWS, 128), 1)
    for w in range(WIN):
        rows = record[w].astype(F32)
        head = jnp.where(lane < offsets[w], rows[:, SAMPLES:], rows[:, :PAD])
        rows = jnp.concatenate([head, rows[:, PAD:SAMPLES]], axis=1)
        rows = rows - jnp.mean(rows, axis=1, keepdims=True)
        rows = rows * lax.rsqrt(jnp.mean(rows * rows, axis=1, keepdims=True) + 1e-06)
        rows = rows.astype(BF16)
        for x in range(NX):
            traces[pl.ds(x * 64 + w * BLK, BLK), :] = rows[x * BLK : (x + 1) * BLK]

    row = lax.broadcasted_iota(jnp.int32, (32, 256), 0)
    col = lax.broadcasted_iota(jnp.int32, (32, 256), 1)
    wanted = jnp.zeros((32, 256), jnp.int32)
    for s in range(NSRC):
        wanted = jnp.where(row % NSRC == s, sources[s], wanted)
    channel = chan * ROWS + (col // 64) * BLK + col % BLK
    same = jnp.logical_and(wanted == channel, row // NSRC == (col // BLK) % 2)
    chosen = dot(jnp.where(same, 1.0, 0.0).astype(BF16), traces[...])
    for j in range(PIECES):
        r, l = j // 8, j % 8
        pieces[j] = chosen[8 * r : 8 * r + 8, 128 * l : 128 * l + 128]

    pl.semaphore_wait(barrier, nchan - 1 + NX - 1 + nz - 1)

    def reduce_copy(to, slot):
        return pltpu.make_async_remote_copy(
            src_ref=pieces.at[pl.ds(to * per, per)],
            dst_ref=reduced.at[slot],
            send_sem=reduce_send.at[to],
            recv_sem=reduce_recv.at[slot],
            device_id=(to, spec),
            device_id_type=MESH,
        )

    @pl.loop(1, nchan)
    def _(step):
        reduce_copy(lax.rem(chan + step, nchan), chan).start()

    reduced[chan] = pieces[pl.ds(chan * per, per)]

    spectrum[...] = dot_t(upper[...], traces[...])
    spectrum[...] += dot_t(lower[...], traces[...])

    @pl.loop(1, nchan)
    def _(step):
        reduce_copy(chan, lax.rem(chan + step, nchan)).wait_recv()

    total = reduced[0]
    for i in range(1, nchan):
        total = total + reduced[i]
    gathered_x[me_x] = total

    def x_copy(to, slot):
        return pltpu.make_async_remote_copy(
            src_ref=gathered_x.at[me_x],
            dst_ref=gathered_x.at[slot],
            send_sem=x_send.at[to],
            recv_sem=x_recv.at[slot],
            device_id=at_x(to),
            device_id_type=MESH,
        )

    for step in (2, 1, 3):
        x_copy(lax.rem(me_x + step, NX), me_x).start()

    chunk = 64
    first_row = lax.broadcasted_iota(jnp.int32, (chunk, 256), 0) == 0
    total = jnp.zeros((1, 256), F32)
    for k in range(0, HALF, chunk):
        re = spectrum[k : k + chunk]
        im = spectrum[HALF + k : HALF + k + chunk]
        size = jnp.sqrt(re * re + im * im)
        if k == 0:
            size = jnp.where(first_row, jnp.abs(re) + jnp.abs(im), size)
        total = total + jnp.sum(size, axis=0, keepdims=True)
    level = WATER * (total / (HALF + 1) + 1e-06)
    low = lax.broadcasted_iota(jnp.int32, (chunk, 128), 1) < 64
    for k in range(0, HALF, chunk):
        re = spectrum[k : k + chunk]
        im = spectrum[HALF + k : HALF + k + chunk]
        size = jnp.sqrt(re * re + im * im)
        if k == 0:
            re = re / (jnp.where(first_row, jnp.abs(re), size) + level)
            im = im / (jnp.where(first_row, jnp.abs(im), size) + level)
        else:
            scale = 1.0 / (size + level)
            re = re * scale
            im = im * scale
        for pair in range(2):
            a = re[:, 128 * pair : 128 * pair + 128]
            b = im[:, 128 * pair : 128 * pair + 128]
            even = jnp.where(low, a, pltpu.roll(b, 64, 1))
            odd = jnp.where(low, pltpu.roll(a, 64, 1), b)
            outgoing[2 * pair, k : k + chunk] = even.astype(BF16)
            outgoing[2 * pair + 1, k : k + chunk] = odd.astype(BF16)

    def white_copy(to, slot):
        return pltpu.make_async_remote_copy(
            src_ref=outgoing.at[to],
            dst_ref=incoming.at[slot],
            send_sem=white_send.at[to],
            recv_sem=white_recv.at[slot],
            device_id=at_x(to),
            device_id_type=MESH,
        )

    for step in (2, 1, 3):
        white_copy(lax.rem(me_x + step, NX), me_x).start()
    incoming[me_x] = outgoing[me_x]

    for step in (2, 1, 3):
        x_copy(me_x, lax.rem(me_x + step, NX)).wait_recv()
    for j in range(per):
        tall = jnp.concatenate([gathered_x[x, j] for x in range(NX)], axis=0)
        piece_out[j] = tall.astype(BF16)

    def chan_copy(to, slot):
        return pltpu.make_async_remote_copy(
            src_ref=piece_out,
            dst_ref=picked.at[pl.ds(slot * per, per)],
            send_sem=chan_send.at[to],
            recv_sem=chan_recv.at[slot],
            device_id=(to, spec),
            device_id_type=MESH,
        )

    @pl.loop(1, nchan)
    def _(step):
        chan_copy(lax.rem(chan + step, nchan), chan).start()

    picked[pl.ds(chan * per, per)] = piece_out[...]

    def widen(x):
        copies[x] = dot(incoming[x], spread[...]).astype(BF16)

    @pl.loop(1, nchan)
    def _(step):
        chan_copy(chan, lax.rem(chan + step, nchan)).wait_recv()

    rows = [
        jnp.concatenate([picked[8 * r + l] for l in range(8)], axis=1) for r in range(4)
    ]
    rows = jnp.concatenate(rows, axis=0)
    both = dot_t(rows, upper[...]) + dot_t(rows, lower[...])
    re = both[:, :HALF]
    im = both[:, HALF:]
    size = jnp.sqrt(re * re + im * im)
    first = lax.broadcasted_iota(jnp.int32, (ROWS, HALF), 1) == 0
    total = jnp.sum(
        jnp.where(first, jnp.abs(re) + jnp.abs(im), size), axis=1, keepdims=True
    )
    level = WATER * (total / (HALF + 1) + 1e-06)
    re = re / (jnp.where(first, jnp.abs(re), size) + level)
    im = im / (jnp.where(first, jnp.abs(im), size) + level)
    parts = []
    for x in range(NX):
        for w in range(WIN):
            tiles = []
            for half in (re, im):
                for big in range(4):
                    for high in range(2):
                        at = 8 * (w * 8 + high * 4 + x)
                        tiles.append(half[at : at + 8, 128 * big : 128 * big + 128])
            parts.append(jnp.concatenate(tiles, axis=0))
    parts = block_transpose(parts)
    for small in range(8):
        a_re = parts[small][:64]
        a_im = parts[small][64:]
        re_b0, re_b1, im_b0, im_b1 = a_re, a_im, -a_im, a_re
        if small == 0:
            shape = (64, 128)
            zero_bin = jnp.logical_and(
                lax.broadcasted_iota(jnp.int32, shape, 0) < 16,
                lax.broadcasted_iota(jnp.int32, shape, 1) % 16 == 0,
            )
            re_b1 = jnp.where(zero_bin, 0.0, re_b1)
            im_b0 = jnp.where(zero_bin, 0.0, im_b0)
            im_b1 = jnp.where(zero_bin, a_im, im_b1)
        left[small, 0, 0] = re_b0.astype(BF16)
        left[small, 0, 1] = re_b1.astype(BF16)
        left[small, 1, 0] = im_b0.astype(BF16)
        left[small, 1, 1] = im_b1.astype(BF16)

    for step in (2, 1, 3):
        white_copy(me_x, lax.rem(me_x + step, NX)).wait_recv()
    for x in range(NX):
        widen(x)

    @pl.loop(0, 8)
    def _(small):
        for big in range(4):
            group = big * 8 + small
            at = pl.ds(pl.multiple_of(group * 16, 16), 16)
            slabs = []
            for p in range(2):
                for x in range(NX):
                    for w in range(WIN):
                        quarter = p * 2 + w
                        tile = copies[x, at, quarter * 128 : quarter * 128 + 128]
                        slabs.append(
                            jnp.concatenate([tile] * 4, axis=1) * mask[...]
                        )
            right = jnp.concatenate(slabs, axis=0)
            rows_left = jnp.concatenate(
                [
                    jnp.concatenate(
                        [left[small, part, p, big * 16 : big * 16 + 16, :] for p in range(2)],
                        axis=1,
                    )
                    for part in range(2)
                ],
                axis=0,
            )
            result = dot(rows_left, right)
            for h in range(4):
                cross[h, pl.ds(group, 32, stride=32), :] = result[:, 128 * h : 128 * h + 128]

    for part in range(2):
        for quad in range(4):
            for h in range(4):
                parts = [
                    cross[h, pl.ds((part * 16 + quad * 4 + i) * 32, 32), :] for i in range(4)
                ]
                parts = block_transpose(parts)
                for j in range(4):
                    at = (part * 16 + h * 4 + j) * 32
                    stacked[at : at + 32, 128 * quad : 128 * quad + 128] = parts[j].astype(BF16)

    def z_copy(step, to, slot):
        return pltpu.make_async_remote_copy(
            src_ref=lags_out.at[step],
            dst_ref=lags_in.at[slot],
            send_sem=z_send.at[step],
            recv_sem=z_recv.at[slot],
            device_id=at_z(to),
            device_id_type=MESH,
        )

    def lag_block(to):
        at = pl.ds(pl.multiple_of(to * lag_rows, lag_rows), lag_rows)
        return dot(inverse[at, :], stacked[...])

    z_steps = sorted(range(1, nz), key=lambda step: -min(step, nz - step))
    for step in z_steps:
        to = lax.rem(me_z + step, nz)
        lags_out[step] = lag_block(to).astype(BF16)
        z_copy(step, to, me_z).start()
    total = lag_block(me_z)
    for step in z_steps[::-1]:
        slot = lax.rem(me_z + step, nz)
        z_copy(step, me_z, slot).wait_recv()
        total = total + lags_in[slot].astype(F32)
    finished[...] = total.astype(BF16)

    own = lag_rows // NX

    def last_copy(to, slot):
        at = pl.ds(pl.multiple_of(to * own, own), own)
        return pltpu.make_async_remote_copy(
            src_ref=finished.at[at],
            dst_ref=last.at[slot],
            send_sem=last_send.at[to],
            recv_sem=last_recv.at[slot],
            device_id=at_x(to),
            device_id_type=MESH,
        )

    for step in (2, 1, 3):
        last_copy(lax.rem(me_x + step, NX), me_x).start()
    last[me_x] = finished[pl.ds(pl.multiple_of(me_x * own, own), own), :]
    for step in (1, 3, 2):
        last_copy(me_x, lax.rem(me_x + step, NX)).wait_recv()
    for quad in range(4):
        parts = [
            last[x, :, 128 * quad : 128 * quad + 128].astype(F32) for x in range(NX)
        ]
        parts = block_transpose(parts)
        for j in range(4):
            s = quad * 4 + j
            out[:, 128 * s : 128 * s + 128] = parts[j].astype(BF16)

    @pl.loop(1, nchan)
    def _(step):
        to = lax.rem(chan + step, nchan)
        reduce_copy(to, chan).wait_send()
        chan_copy(to, chan).wait_send()

    for step in (1, 2, 3):
        to = lax.rem(me_x + step, NX)
        x_copy(to, me_x).wait_send()
        white_copy(to, me_x).wait_send()
        last_copy(to, me_x).wait_send()
    for step in z_steps:
        z_copy(step, lax.rem(me_z + step, nz), me_z).wait_send()


def local(nchan, nz, record, offsets, sources):
    lag_rows = HALF // nz
    own = lag_rows // NX
    per = PIECES // nchan
    upper, lower = forward_tables()
    inverse = inverse_table(nz * NX * WIN)
    vmem = pl.BlockSpec(memory_space=pltpu.VMEM)
    smem = pl.BlockSpec(memory_space=pltpu.SMEM)
    dma = pltpu.SemaphoreType.DMA
    flat = pl.pallas_call(
        functools.partial(kernel, nchan, nz),
        out_shape=jax.ShapeDtypeStruct((own, NSRC * ROWS), BF16),
        in_specs=[smem, smem] + [vmem] * 6,
        out_specs=vmem,
        scratch_shapes=[
            pltpu.VMEM((256, SAMPLES), BF16),
            pltpu.VMEM((PIECES, 8, 128), F32),
            pltpu.VMEM((nchan, per, 8, 128), F32),
            pltpu.VMEM((NX, per, 8, 128), F32),
            pltpu.VMEM((per, 32, 128), BF16),
            pltpu.VMEM((PIECES, 32, 128), BF16),
            pltpu.VMEM((SAMPLES, 256), F32),
            pltpu.VMEM((NX, HALF, 128), BF16),
            pltpu.VMEM((NX, HALF, 128), BF16),
            pltpu.VMEM((8, 2, 2, 64, 128), BF16),
            pltpu.VMEM((NX, HALF, 512), BF16),
            pltpu.VMEM((4, SAMPLES, 128), F32),
            pltpu.VMEM((SAMPLES, 512), BF16),
            pltpu.VMEM((nz, lag_rows, 512), BF16),
            pltpu.VMEM((nz, lag_rows, 512), BF16),
            pltpu.VMEM((lag_rows, 512), BF16),
            pltpu.VMEM((NX, own, 512), BF16),
            dma((nchan,)),
            dma((nchan,)),
            dma((NX,)),
            dma((NX,)),
            dma((nchan,)),
            dma((nchan,)),
            dma((NX,)),
            dma((NX,)),
            dma((nz,)),
            dma((nz,)),
            dma((NX,)),
            dma((NX,)),
        ],
        compiler_params=pltpu.CompilerParams(
            collective_id=0, has_side_effects=True, vmem_limit_bytes=48 * 1024 * 1024
        ),
        cost_estimate=pl.CostEstimate(
            flops=3 * 10**9, bytes_accessed=7 * 10**6, transcendentals=10**6
        ),
    )(
        offsets,
        sources,
        jnp.transpose(record, (1, 0, 2)),
        jnp.asarray(upper),
        jnp.asarray(lower),
        jnp.asarray(inverse),
        jnp.asarray(spread_table()),
        jnp.asarray(diagonal_mask()),
    )
    return flat.reshape(own, NSRC, ROWS)


def solution(mesh):
    nchan = mesh.shape["chan"]
    nz = mesh.shape["spec"] // NX
    in_specs = (P("chan", "spec", None), P("spec"), P())
    out_specs = P("spec", None, "chan")
    return jax.shard_map(
        functools.partial(local, nchan, nz),
        mesh=mesh,
        in_specs=in_specs,
        out_specs=out_specs,
        check_vma=False,
    )
```

profile of v0, /device:TPU:1, one launch (start us, length us, event | category | flops | bytes accessed | tf_op | source)
XLA Modules:
  0.0 73.1 jit_solution(11806634983900354158)
XLA Ops:
  0.0 1.1 %copy.12 = bf16[128,2,1152]{2,0,1:T(8,128)(2,1)S(1)} copy(bf16[128,2,1152]{2,1,0:T(2,128)(2,1)} %param.8) | data formatting | bytes 1179648 | tf_op args[0]
  1.1 0.0 copy-start
  1.1 0.6 copy-done
  1.8 0.0 copy-start.1
  1.8 0.7 copy-done.1
  2.4 0.0 copy-start.2
  2.4 1.6 %copy-done.2 = bf16[1024,1024]{1,0:T(8,128)(2,1)S(1)} copy-done((bf16[1024,1024]{1,0:T(8,128)(2,1)S(1)}, bf16[1024,1024]{1,0:T(8,128)(2,1)}, u32[]{:S(2)}) %copy-start.2) | copy-done | bytes 2097176
  4.0 0.0 copy-start.3
  4.0 1.6 %copy-done.3 = bf16[1024,1024]{1,0:T(8,128)(2,1)S(1)} copy-done((bf16[1024,1024]{1,0:T(8,128)(2,1)S(1)}, bf16[1024,1024]{1,0:T(8,128)(2,1)}, u32[]{:S(2)}) %copy-start.3) | copy-done | bytes 2097176
  5.6 0.0 copy-start.4
  5.6 1.2 %copy-done.4 = bf16[512,1024]{1,0:T(8,128)(2,1)S(1)} copy-done((bf16[512,1024]{1,0:T(8,128)(2,1)S(1)}, bf16[512,1024]{1,0:T(8,128)(2,1)}, u32[]{:S(2)}) %copy-start.4) | copy-done | bytes 1048600
  6.9 0.0 copy-start.5
  6.9 0.9 %copy-done.5 = bf16[128,512]{1,0:T(8,128)(2,1)S(1)} copy-done((bf16[128,512]{1,0:T(8,128)(2,1)S(1)}, bf16[128,512]{1,0:T(8,128)(2,1)}, u32[]{:S(2)}) %copy-start.5) | copy-done | bytes 131096
  7.8 0.0 copy-start.6
  7.8 0.7 copy-done.6
  8.5 64.0 %shard_map.82 = bf16[32,2048]{1,0:T(8,128)(2,1)S(1)} custom-call(s32[2]{0:T(128)S(1)} %copy-done, s32[16]{0:T(128)S(1)} %copy-done.1, bf16[2,128,1152]{2,1,0:T(8,128)(2,1)S(1)} %bitcast.5, bf16[1024,1024]{1,0:T(8,128)(2,1)S(1)} %copy-done.3, bf16[1024,1024]{1,0:T(8,128)(2,1)S(1)} %copy-done.2, bf16[512,1024]{1,0:T(8,128)(2,1)S(1)} %copy-done.4, ...), custom_call_target="tpu_custom_call" | custom-call | flops 3000000000 | bytes 7000000 | tf_op jit(solution)/shard_map/pallas_call | solution.py:474
  72.4 0.7 copy.10
Async XLA Ops:
  1.1 0.7 copy-start
  1.8 0.7 copy-start.1
  2.4 1.6 %copy-start.2 = (bf16[1024,1024]{1,0:T(8,128)(2,1)S(1)}, bf16[1024,1024]{1,0:T(8,128)(2,1)}, u32[]{:S(2)}) copy-start(bf16[1024,1024]{1,0:T(8,128)(2,1)} %constant.11.clone.lower) | copy-start | bytes 6291460
  4.0 1.6 %copy-start.3 = (bf16[1024,1024]{1,0:T(8,128)(2,1)S(1)}, bf16[1024,1024]{1,0:T(8,128)(2,1)}, u32[]{:S(2)}) copy-start(bf16[1024,1024]{1,0:T(8,128)(2,1)} %constant.10.clone.upper) | copy-start | bytes 6291460
  5.6 1.2 %copy-start.4 = (bf16[512,1024]{1,0:T(8,128)(2,1)S(1)}, bf16[512,1024]{1,0:T(8,128)(2,1)}, u32[]{:S(2)}) copy-start(bf16[512,1024]{1,0:T(8,128)(2,1)} %constant.12.clone.inverse) | copy-start | bytes 3145732
  6.9 0.9 %copy-start.5 = (bf16[128,512]{1,0:T(8,128)(2,1)S(1)}, bf16[128,512]{1,0:T(8,128)(2,1)}, u32[]{:S(2)}) copy-start(bf16[128,512]{1,0:T(8,128)(2,1)} %constant.13.clone.spread) | copy-start | bytes 393220
  7.8 0.7 copy-start.6
where the time goes:
time: 73.5 us; the launch traced here: 73.1 us
  Pallas kernels  64 us (87%)
  local copies, waits for them, and re-layouts  9.13 us (12%)
    pallas_call x1, Pallas kernels, local(): pl.pallas_call(functools.partial(kernel, nchan, nz), out_shape=jax.ShapeD...  64 us
    unnamed x16, local copies, waits for them, and re-layouts  9.13 us

commit v1 on v0

--- a/solution.py
+++ b/solution.py
@@ -19,7 +19,7 @@
 WIN = 2
 BLK = ROWS // NX
 GROUPS = 32
-PIECES = 32
+LANES = SAMPLES // 128
 F32 = jnp.float32
 BF16 = jnp.bfloat16
 MESH = pl.DeviceIdType.MESH
@@ -50,18 +50,9 @@
     return table.astype(jnp.bfloat16)
 
 
-def spread_table():
-    table = np.zeros((4, BLK, 4, 4, BLK))
-    for quarter in range(4):
-        for copy in range(4):
-            table[quarter, np.arange(BLK), quarter, copy, np.arange(BLK)] = 1.0
-    return table.reshape(128, 512).astype(jnp.bfloat16)
-
-
-def diagonal_mask():
-    mask = np.zeros((16, 16, BLK))
-    mask[np.arange(16), np.arange(16)] = 1.0
-    return mask.reshape(16, 512).astype(jnp.bfloat16)
+def split_chan(nchan):
+    nlow = 2 if nchan >= 8 else 1
+    return nlow, nchan // (2 * nlow)
 
 
 def dot_t(left, right):
@@ -93,19 +84,22 @@
 def kernel(
     nchan,
     nz,
+    offsets_hbm,
+    sources_hbm,
+    record,
+    upper_hbm,
+    lower_hbm,
+    inverse_hbm,
+    out,
     offsets,
     sources,
-    record,
     upper,
     lower,
     inverse,
-    spread,
-    mask,
-    out,
     traces,
     pieces,
     reduced,
-    gathered_x,
+    gathered,
     piece_out,
     picked,
     spectrum,
@@ -119,12 +113,15 @@
     lags_in,
     finished,
     last,
+    load_sem,
     reduce_send,
     reduce_recv,
-    x_send,
-    x_recv,
-    chan_send,
-    chan_recv,
+    side_send,
+    side_recv,
+    y_send,
+    y_recv,
+    core_send,
+    core_recv,
     white_send,
     white_recv,
     z_send,
@@ -132,12 +129,26 @@
     last_send,
     last_recv,
 ):
+    nlow, ny = split_chan(nchan)
+    per = LANES // ny
+    lag_rows = HALF // nz
+    plane = 2 * ny
+    side = nlow * NX
     chan = lax.axis_index("chan")
     spec = lax.axis_index("spec")
     me_x = lax.rem(spec, NX)
     me_z = spec // NX
-    per = PIECES // nchan
-    lag_rows = HALF // nz
+    me_low = chan // plane
+    me_plane = lax.rem(chan, plane)
+    me_y = me_plane // 2
+    me_core = lax.rem(chan, 2)
+    me_side = me_low * NX + me_x
+
+    def at_plane(other):
+        return (me_low * plane + other, spec)
+
+    def at_side(other):
+        return (other // NX * plane + me_plane, me_z * NX + lax.rem(other, NX))
 
     def at_x(other):
         return (chan, me_z * NX + other)
@@ -145,18 +156,33 @@
     def at_z(other):
         return (chan, other * NX + me_x)
 
+    loads = [
+        pltpu.make_async_copy(source, target, load_sem.at[i])
+        for i, (source, target) in enumerate(
+            [
+                (offsets_hbm, offsets),
+                (sources_hbm, sources),
+                (upper_hbm, upper),
+                (lower_hbm, lower),
+                (inverse_hbm, inverse),
+            ]
+        )
+    ]
+    for load in loads:
+        load.start()
+
     barrier = pltpu.get_barrier_semaphore()
 
-    @pl.loop(1, nchan)
+    @pl.loop(1, plane)
     def _(step):
         pl.semaphore_signal(
-            barrier, inc=1, device_id=(lax.rem(chan + step, nchan), spec), device_id_type=MESH
-        )
-
-    @pl.loop(1, NX)
+            barrier, inc=1, device_id=at_plane(lax.rem(me_plane + step, plane)), device_id_type=MESH
+        )
+
+    @pl.loop(1, side)
     def _(step):
         pl.semaphore_signal(
-            barrier, inc=1, device_id=at_x(lax.rem(me_x + step, NX)), device_id_type=MESH
+            barrier, inc=1, device_id=at_side(lax.rem(me_side + step, side)), device_id_type=MESH
         )
 
     @pl.loop(1, nz)
@@ -164,6 +190,9 @@
         pl.semaphore_signal(
             barrier, inc=1, device_id=at_z(lax.rem(me_z + step, nz)), device_id_type=MESH
         )
+
+    loads[0].wait()
+    loads[1].wait()
 
     lane = lax.broadcasted_iota(jnp.int32, (ROWS, 128), 1)
     for w in range(WIN):
@@ -184,52 +213,56 @@
     channel = chan * ROWS + (col // 64) * BLK + col % BLK
     same = jnp.logical_and(wanted == channel, row // NSRC == (col // BLK) % 2)
     chosen = dot(jnp.where(same, 1.0, 0.0).astype(BF16), traces[...])
-    for j in range(PIECES):
-        r, l = j // 8, j % 8
-        pieces[j] = chosen[8 * r : 8 * r + 8, 128 * l : 128 * l + 128]
-
-    pl.semaphore_wait(barrier, nchan - 1 + NX - 1 + nz - 1)
+    chosen = chosen.astype(BF16)
+    for w in range(WIN):
+        for l in range(LANES):
+            pieces[w, l] = chosen[NSRC * w : NSRC * w + NSRC, 128 * l : 128 * l + 128]
+
+    pl.semaphore_wait(barrier, plane - 1 + side - 1 + nz - 1)
 
     def reduce_copy(to, slot):
         return pltpu.make_async_remote_copy(
-            src_ref=pieces.at[pl.ds(to * per, per)],
+            src_ref=pieces.at[lax.rem(to, 2), pl.ds(to // 2 * per, per)],
             dst_ref=reduced.at[slot],
             send_sem=reduce_send.at[to],
             recv_sem=reduce_recv.at[slot],
-            device_id=(to, spec),
+            device_id=at_plane(to),
             device_id_type=MESH,
         )
 
-    @pl.loop(1, nchan)
-    def _(step):
-        reduce_copy(lax.rem(chan + step, nchan), chan).start()
-
-    reduced[chan] = pieces[pl.ds(chan * per, per)]
+    @pl.loop(1, plane)
+    def _(step):
+        reduce_copy(lax.rem(me_plane + step, plane), me_plane).start()
+
+    reduced[me_plane] = pieces[me_core, pl.ds(me_y * per, per)]
+    loads[2].wait()
+    loads[3].wait()
 
     spectrum[...] = dot_t(upper[...], traces[...])
     spectrum[...] += dot_t(lower[...], traces[...])
 
-    @pl.loop(1, nchan)
-    def _(step):
-        reduce_copy(chan, lax.rem(chan + step, nchan)).wait_recv()
-
-    total = reduced[0]
-    for i in range(1, nchan):
-        total = total + reduced[i]
-    gathered_x[me_x] = total
-
-    def x_copy(to, slot):
+    @pl.loop(1, plane)
+    def _(step):
+        reduce_copy(me_plane, lax.rem(me_plane + step, plane)).wait_recv()
+
+    total = reduced[0].astype(F32)
+    for i in range(1, plane):
+        total = total + reduced[i].astype(F32)
+    gathered[me_side] = total.astype(BF16)
+
+    def side_copy(to, slot):
         return pltpu.make_async_remote_copy(
-            src_ref=gathered_x.at[me_x],
-            dst_ref=gathered_x.at[slot],
-            send_sem=x_send.at[to],
-            recv_sem=x_recv.at[slot],
-            device_id=at_x(to),
+            src_ref=gathered.at[me_side],
+            dst_ref=gathered.at[slot],
+            send_sem=side_send.at[to],
+            recv_sem=side_recv.at[slot],
+            device_id=at_side(to),
             device_id_type=MESH,
         )
 
-    for step in (2, 1, 3):
-        x_copy(lax.rem(me_x + step, NX), me_x).start()
+    @pl.loop(1, side)
+    def _(step):
+        side_copy(lax.rem(me_side + step, side), me_side).start()
 
     chunk = 64
     first_row = lax.broadcasted_iota(jnp.int32, (chunk, 256), 0) == 0
@@ -276,37 +309,68 @@
         white_copy(lax.rem(me_x + step, NX), me_x).start()
     incoming[me_x] = outgoing[me_x]
 
-    for step in (2, 1, 3):
-        x_copy(me_x, lax.rem(me_x + step, NX)).wait_recv()
-    for j in range(per):
-        tall = jnp.concatenate([gathered_x[x, j] for x in range(NX)], axis=0)
-        piece_out[j] = tall.astype(BF16)
-
-    def chan_copy(to, slot):
+    @pl.loop(1, side)
+    def _(step):
+        side_copy(me_side, lax.rem(me_side + step, side)).wait_recv()
+
+    for l in range(per):
+        for x in range(NX):
+            total = gathered[x, l].astype(F32)
+            for low_z in range(1, nlow):
+                total = total + gathered[low_z * NX + x, l].astype(F32)
+            piece_out[l, NSRC * x : NSRC * x + NSRC] = total.astype(BF16)
+
+    def y_copy(to, slot):
         return pltpu.make_async_remote_copy(
             src_ref=piece_out,
-            dst_ref=picked.at[pl.ds(slot * per, per)],
-            send_sem=chan_send.at[to],
-            recv_sem=chan_recv.at[slot],
-            device_id=(to, spec),
+            dst_ref=picked.at[me_core, pl.ds(slot * per, per)],
+            send_sem=y_send.at[to],
+            recv_sem=y_recv.at[slot],
+            device_id=at_plane(to * 2 + me_core),
             device_id_type=MESH,
         )
 
-    @pl.loop(1, nchan)
-    def _(step):
-        chan_copy(lax.rem(chan + step, nchan), chan).start()
-
-    picked[pl.ds(chan * per, per)] = piece_out[...]
+    def core_copy(core, slot):
+        at = picked.at[core, pl.ds(slot * per, per)]
+        return pltpu.make_async_remote_copy(
+            src_ref=at,
+            dst_ref=at,
+            send_sem=core_send.at[slot],
+            recv_sem=core_recv.at[slot],
+            device_id=at_plane(me_y * 2 + 1 - me_core),
+            device_id_type=MESH,
+        )
+
+    @pl.loop(1, ny)
+    def _(step):
+        y_copy(lax.rem(me_y + step, ny), me_y).start()
+
+    picked[me_core, pl.ds(me_y * per, per)] = piece_out[...]
+    core_copy(me_core, me_y).start()
+
+    @pl.loop(1, ny)
+    def _(step):
+        slot = lax.rem(me_y + step, ny)
+        y_copy(me_y, slot).wait_recv()
+        core_copy(me_core, slot).start()
+
+    r = lax.broadcasted_iota(jnp.int32, (128, 512), 0)
+    c = lax.broadcasted_iota(jnp.int32, (128, 512), 1)
+    match = jnp.logical_and(r // BLK == c // 128, r % BLK == c % BLK)
+    spread = jnp.where(match, 1.0, 0.0).astype(BF16)
+    r = lax.broadcasted_iota(jnp.int32, (16, 512), 0)
+    c = lax.broadcasted_iota(jnp.int32, (16, 512), 1)
+    mask = jnp.where(r == c // BLK, 1.0, 0.0).astype(BF16)
 
     def widen(x):
-        copies[x] = dot(incoming[x], spread[...]).astype(BF16)
-
-    @pl.loop(1, nchan)
-    def _(step):
-        chan_copy(chan, lax.rem(chan + step, nchan)).wait_recv()
+        copies[x] = dot(incoming[x], spread).astype(BF16)
+
+    @pl.loop(0, ny)
+    def _(slot):
+        core_copy(1 - me_core, slot).wait_recv()
 
     rows = [
-        jnp.concatenate([picked[8 * r + l] for l in range(8)], axis=1) for r in range(4)
+        jnp.concatenate([picked[w, l] for l in range(LANES)], axis=1) for w in range(WIN)
     ]
     rows = jnp.concatenate(rows, axis=0)
     both = dot_t(rows, upper[...]) + dot_t(rows, lower[...])
@@ -326,9 +390,8 @@
             tiles = []
             for half in (re, im):
                 for big in range(4):
-                    for high in range(2):
-                        at = 8 * (w * 8 + high * 4 + x)
-                        tiles.append(half[at : at + 8, 128 * big : 128 * big + 128])
+                    at = NSRC * (w * NX + x)
+                    tiles.append(half[at : at + NSRC, 128 * big : 128 * big + 128])
             parts.append(jnp.concatenate(tiles, axis=0))
     parts = block_transpose(parts)
     for small in range(8):
@@ -366,7 +429,7 @@
                         quarter = p * 2 + w
                         tile = copies[x, at, quarter * 128 : quarter * 128 + 128]
                         slabs.append(
-                            jnp.concatenate([tile] * 4, axis=1) * mask[...]
+                            jnp.concatenate([tile] * 4, axis=1) * mask
                         )
             right = jnp.concatenate(slabs, axis=0)
             rows_left = jnp.concatenate(
@@ -394,6 +457,8 @@
                     at = (part * 16 + h * 4 + j) * 32
                     stacked[at : at + 32, 128 * quad : 128 * quad + 128] = parts[j].astype(BF16)
 
+    loads[4].wait()
+
     def z_copy(step, to, slot):
         return pltpu.make_async_remote_copy(
             src_ref=lags_out.at[step],
@@ -447,15 +512,24 @@
             s = quad * 4 + j
             out[:, 128 * s : 128 * s + 128] = parts[j].astype(BF16)
 
-    @pl.loop(1, nchan)
-    def _(step):
-        to = lax.rem(chan + step, nchan)
-        reduce_copy(to, chan).wait_send()
-        chan_copy(to, chan).wait_send()
+    @pl.loop(1, plane)
+    def _(step):
+        reduce_copy(lax.rem(me_plane + step, plane), me_plane).wait_send()
+
+    @pl.loop(1, side)
+    def _(step):
+        side_copy(lax.rem(me_side + step, side), me_side).wait_send()
+
+    @pl.loop(1, ny)
+    def _(step):
+        y_copy(lax.rem(me_y + step, ny), me_y).wait_send()
+
+    @pl.loop(0, ny)
+    def _(slot):
+        core_copy(me_core, slot).wait_send()
 
     for step in (1, 2, 3):
         to = lax.rem(me_x + step, NX)
-        x_copy(to, me_x).wait_send()
         white_copy(to, me_x).wait_send()
         last_copy(to, me_x).wait_send()
     for step in z_steps:
@@ -465,24 +539,30 @@
 def local(nchan, nz, record, offsets, sources):
     lag_rows = HALF // nz
     own = lag_rows // NX
-    per = PIECES // nchan
+    nlow, ny = split_chan(nchan)
+    per = LANES // ny
     upper, lower = forward_tables()
     inverse = inverse_table(nz * NX * WIN)
     vmem = pl.BlockSpec(memory_space=pltpu.VMEM)
-    smem = pl.BlockSpec(memory_space=pltpu.SMEM)
+    hbm = pl.BlockSpec(memory_space=pltpu.HBM)
     dma = pltpu.SemaphoreType.DMA
     flat = pl.pallas_call(
         functools.partial(kernel, nchan, nz),
         out_shape=jax.ShapeDtypeStruct((own, NSRC * ROWS), BF16),
-        in_specs=[smem, smem] + [vmem] * 6,
+        in_specs=[hbm, hbm, vmem, hbm, hbm, hbm],
         out_specs=vmem,
         scratch_shapes=[
+            pltpu.SMEM((WIN,), jnp.int32),
+            pltpu.SMEM((NSRC,), jnp.int32),
+            pltpu.VMEM((SAMPLES, SAMPLES), BF16),
+            pltpu.VMEM((SAMPLES, SAMPLES), BF16),
+            pltpu.VMEM((HALF, SAMPLES), BF16),
             pltpu.VMEM((256, SAMPLES), BF16),
-            pltpu.VMEM((PIECES, 8, 128), F32),
-            pltpu.VMEM((nchan, per, 8, 128), F32),
-            pltpu.VMEM((NX, per, 8, 128), F32),
-            pltpu.VMEM((per, 32, 128), BF16),
-            pltpu.VMEM((PIECES, 32, 128), BF16),
+            pltpu.VMEM((WIN, LANES, NSRC, 128), BF16),
+            pltpu.VMEM((2 * ny, per, NSRC, 128), BF16),
+            pltpu.VMEM((nlow * NX, per, NSRC, 128), BF16),
+            pltpu.VMEM((per, NX * NSRC, 128), BF16),
+            pltpu.VMEM((WIN, LANES, NX * NSRC, 128), BF16),
             pltpu.VMEM((SAMPLES, 256), F32),
             pltpu.VMEM((NX, HALF, 128), BF16),
             pltpu.VMEM((NX, HALF, 128), BF16),
@@ -494,12 +574,15 @@
             pltpu.VMEM((nz, lag_rows, 512), BF16),
             pltpu.VMEM((lag_rows, 512), BF16),
             pltpu.VMEM((NX, own, 512), BF16),
-            dma((nchan,)),
-            dma((nchan,)),
-            dma((NX,)),
-            dma((NX,)),
-            dma((nchan,)),
-            dma((nchan,)),
+            dma((5,)),
+            dma((2 * ny,)),
+            dma((2 * ny,)),
+            dma((nlow * NX,)),
+            dma((nlow * NX,)),
+            dma((ny,)),
+            dma((ny,)),
+            dma((ny,)),
+            dma((ny,)),
             dma((NX,)),
             dma((NX,)),
             dma((nz,)),
@@ -520,8 +603,6 @@
         jnp.asarray(upper),
         jnp.asarray(lower),
         jnp.asarray(inverse),
-        jnp.asarray(spread_table()),
-        jnp.asarray(diagonal_mask()),
     )
     return flat.reshape(own, NSRC, ROWS)
 

time: 73.5 us -> 68.6 us (0.933)
  Pallas kernels: 64 us -> 60.8 us
  local copies, waits for them, and re-layouts: 9.13 us -> 7.51 us
    pallas_call x1, Pallas kernels: 64 us -> 60.8 us  [local(): pl.pallas_call(functools.partial(kernel, nchan, nz), out_shape=jax.ShapeD...]
    unnamed x16 -> x12, local copies, waits for them, and re-layouts: 9.13 us -> 7.51 us
where the time goes in v1:
time: 68.6 us; the launch traced here: 68.4 us
  Pallas kernels  60.8 us (89%)
  local copies, waits for them, and re-layouts  7.51 us (11%)
    pallas_call x1, Pallas kernels, local(): pl.pallas_call(functools.partial(kernel, nchan, nz), out_shape=jax.ShapeD...  60.8 us
    unnamed x12, local copies, waits for them, and re-layouts  7.51 us

profile of v1, /device:TPU:1, one launch (start us, length us, event | category | flops | bytes accessed | tf_op | source)
XLA Modules:
  0.0 68.4 jit_solution(133653381238663596)
XLA Ops:
  0.0 1.1 %copy.10 = bf16[128,2,1152]{2,0,1:T(8,128)(2,1)S(1)} copy(bf16[128,2,1152]{2,1,0:T(2,128)(2,1)} %param.6) | data formatting | bytes 1179648 | tf_op args[0]
  1.1 0.0 copy-start
  1.1 0.6 copy-done
  1.8 0.0 copy-start.1
  1.8 0.7 copy-done.1
  2.4 0.0 copy-start.2
  2.4 1.6 %copy-done.2 = bf16[1024,1024]{1,0:T(8,128)(2,1)S(1)} copy-done((bf16[1024,1024]{1,0:T(8,128)(2,1)S(1)}, bf16[1024,1024]{1,0:T(8,128)(2,1)}, u32[]{:S(2)}) %copy-start.2) | copy-done | bytes 2097176
  4.0 0.0 copy-start.3
  4.0 1.6 %copy-done.3 = bf16[1024,1024]{1,0:T(8,128)(2,1)S(1)} copy-done((bf16[1024,1024]{1,0:T(8,128)(2,1)S(1)}, bf16[1024,1024]{1,0:T(8,128)(2,1)}, u32[]{:S(2)}) %copy-start.3) | copy-done | bytes 2097176
  5.6 0.0 copy-start.4
  5.6 1.2 %copy-done.4 = bf16[512,1024]{1,0:T(8,128)(2,1)S(1)} copy-done((bf16[512,1024]{1,0:T(8,128)(2,1)S(1)}, bf16[512,1024]{1,0:T(8,128)(2,1)}, u32[]{:S(2)}) %copy-start.4) | copy-done | bytes 1048600
  6.9 60.8 %shard_map.64 = bf16[32,2048]{1,0:T(8,128)(2,1)S(1)} custom-call(s32[2]{0:T(128)S(1)} %copy-done, s32[16]{0:T(128)S(1)} %copy-done.1, bf16[2,128,1152]{2,1,0:T(8,128)(2,1)S(1)} %bitcast.5, bf16[1024,1024]{1,0:T(8,128)(2,1)S(1)} %copy-done.3, bf16[1024,1024]{1,0:T(8,128)(2,1)S(1)} %copy-done.2, bf16[512,1024]{1,0:T(8,128)(2,1)S(1)} %copy-done.4), custom_call_target="tpu_custom_call" | custom-call | flops 3000000000 | bytes 7000000 | tf_op jit(solution)/shard_map/pallas_call | solution.py:549
  67.7 0.7 copy.8
Async XLA Ops:
  1.1 0.7 copy-start
  1.8 0.7 copy-start.1
  2.4 1.6 %copy-start.2 = (bf16[1024,1024]{1,0:T(8,128)(2,1)S(1)}, bf16[1024,1024]{1,0:T(8,128)(2,1)}, u32[]{:S(2)}) copy-start(bf16[1024,1024]{1,0:T(8,128)(2,1)} %constant.7.clone.lower_hbm) | copy-start | bytes 6291460
  4.0 1.6 %copy-start.3 = (bf16[1024,1024]{1,0:T(8,128)(2,1)S(1)}, bf16[1024,1024]{1,0:T(8,128)(2,1)}, u32[]{:S(2)}) copy-start(bf16[1024,1024]{1,0:T(8,128)(2,1)} %constant.6.clone.upper_hbm) | copy-start | bytes 6291460
  5.6 1.2 %copy-start.4 = (bf16[512,1024]{1,0:T(8,128)(2,1)S(1)}, bf16[512,1024]{1,0:T(8,128)(2,1)}, u32[]{:S(2)}) copy-start(bf16[512,1024]{1,0:T(8,128)(2,1)} %constant.8.clone.inverse_hbm) | copy-start | bytes 3145732

commit v2 on v1

--- a/solution.py
+++ b/solution.py
@@ -20,6 +20,9 @@
 BLK = ROWS // NX
 GROUPS = 32
 LANES = SAMPLES // 128
+NZ = 4
+CHUNKS = 2
+WIDE = NSRC * BLK // CHUNKS
 F32 = jnp.float32
 BF16 = jnp.bfloat16
 MESH = pl.DeviceIdType.MESH
@@ -65,34 +68,30 @@
 
 def block_transpose(parts):
     count = len(parts)
+    width = 128 // count
     lane = lax.broadcasted_iota(jnp.int32, parts[0].shape, 1)
-    step = count // 2
-    while step:
-        width = step * 128 // count
-        low = (lane // width) % 2 == 0
-        done = list(parts)
-        for i in range(count):
-            if (i // step) % 2 == 0:
-                a, b = parts[i], parts[i + step]
-                done[i] = jnp.where(low, a, pltpu.roll(b, width, 1))
-                done[i + step] = jnp.where(low, pltpu.roll(a, 128 - width, 1), b)
-        parts = done
-        step //= 2
-    return parts
+    masks = [lane // width == i for i in range(count - 1)]
+
+    def pick(choices):
+        result = choices[-1]
+        for mask, choice in zip(masks, choices):
+            result = jnp.where(mask, choice, result)
+        return result
+
+    turned = []
+    for d in range(count):
+        part = pick([parts[(i - d) % count] for i in range(count)])
+        turned.append(pltpu.roll(part, 128 - width * d, 1) if d else part)
+    return [pick([turned[(j - i) % count] for i in range(count)]) for j in range(count)]
 
 
 def kernel(
     nchan,
-    nz,
-    offsets_hbm,
-    sources_hbm,
+    numbers_hbm,
     record,
-    upper_hbm,
-    lower_hbm,
-    inverse_hbm,
+    tables_hbm,
     out,
-    offsets,
-    sources,
+    numbers,
     upper,
     lower,
     inverse,
@@ -107,9 +106,12 @@
     incoming,
     left,
     copies,
+    right,
     cross,
     stacked,
     lags_out,
+    mixed,
+    kept,
     lags_in,
     finished,
     last,
@@ -131,7 +133,6 @@
 ):
     nlow, ny = split_chan(nchan)
     per = LANES // ny
-    lag_rows = HALF // nz
     plane = 2 * ny
     side = nlow * NX
     chan = lax.axis_index("chan")
@@ -160,11 +161,10 @@
         pltpu.make_async_copy(source, target, load_sem.at[i])
         for i, (source, target) in enumerate(
             [
-                (offsets_hbm, offsets),
-                (sources_hbm, sources),
-                (upper_hbm, upper),
-                (lower_hbm, lower),
-                (inverse_hbm, inverse),
+                (numbers_hbm, numbers),
+                (tables_hbm.at[pl.ds(0, SAMPLES)], upper),
+                (tables_hbm.at[pl.ds(SAMPLES, SAMPLES)], lower),
+                (tables_hbm.at[pl.ds(2 * SAMPLES, HALF)], inverse),
             ]
         )
     ]
@@ -185,19 +185,17 @@
             barrier, inc=1, device_id=at_side(lax.rem(me_side + step, side)), device_id_type=MESH
         )
 
-    @pl.loop(1, nz)
-    def _(step):
+    for step in (1, NZ - 1):
         pl.semaphore_signal(
-            barrier, inc=1, device_id=at_z(lax.rem(me_z + step, nz)), device_id_type=MESH
+            barrier, inc=1, device_id=at_z(lax.rem(me_z + step, NZ)), device_id_type=MESH
         )
 
     loads[0].wait()
-    loads[1].wait()
 
     lane = lax.broadcasted_iota(jnp.int32, (ROWS, 128), 1)
     for w in range(WIN):
         rows = record[w].astype(F32)
-        head = jnp.where(lane < offsets[w], rows[:, SAMPLES:], rows[:, :PAD])
+        head = jnp.where(lane < numbers[w], rows[:, SAMPLES:], rows[:, :PAD])
         rows = jnp.concatenate([head, rows[:, PAD:SAMPLES]], axis=1)
         rows = rows - jnp.mean(rows, axis=1, keepdims=True)
         rows = rows * lax.rsqrt(jnp.mean(rows * rows, axis=1, keepdims=True) + 1e-06)
@@ -209,7 +207,7 @@
     col = lax.broadcasted_iota(jnp.int32, (32, 256), 1)
     wanted = jnp.zeros((32, 256), jnp.int32)
     for s in range(NSRC):
-        wanted = jnp.where(row % NSRC == s, sources[s], wanted)
+        wanted = jnp.where(row % NSRC == s, numbers[WIN + s], wanted)
     channel = chan * ROWS + (col // 64) * BLK + col % BLK
     same = jnp.logical_and(wanted == channel, row // NSRC == (col // BLK) % 2)
     chosen = dot(jnp.where(same, 1.0, 0.0).astype(BF16), traces[...])
@@ -218,7 +216,7 @@
         for l in range(LANES):
             pieces[w, l] = chosen[NSRC * w : NSRC * w + NSRC, 128 * l : 128 * l + 128]
 
-    pl.semaphore_wait(barrier, plane - 1 + side - 1 + nz - 1)
+    pl.semaphore_wait(barrier, plane - 1 + side - 1 + 2)
 
     def reduce_copy(to, slot):
         return pltpu.make_async_remote_copy(
@@ -235,34 +233,11 @@
         reduce_copy(lax.rem(me_plane + step, plane), me_plane).start()
 
     reduced[me_plane] = pieces[me_core, pl.ds(me_y * per, per)]
+    loads[1].wait()
     loads[2].wait()
-    loads[3].wait()
 
     spectrum[...] = dot_t(upper[...], traces[...])
     spectrum[...] += dot_t(lower[...], traces[...])
-
-    @pl.loop(1, plane)
-    def _(step):
-        reduce_copy(me_plane, lax.rem(me_plane + step, plane)).wait_recv()
-
-    total = reduced[0].astype(F32)
-    for i in range(1, plane):
-        total = total + reduced[i].astype(F32)
-    gathered[me_side] = total.astype(BF16)
-
-    def side_copy(to, slot):
-        return pltpu.make_async_remote_copy(
-            src_ref=gathered.at[me_side],
-            dst_ref=gathered.at[slot],
-            send_sem=side_send.at[to],
-            recv_sem=side_recv.at[slot],
-            device_id=at_side(to),
-            device_id_type=MESH,
-        )
-
-    @pl.loop(1, side)
-    def _(step):
-        side_copy(lax.rem(me_side + step, side), me_side).start()
 
     chunk = 64
     first_row = lax.broadcasted_iota(jnp.int32, (chunk, 256), 0) == 0
@@ -309,6 +284,29 @@
         white_copy(lax.rem(me_x + step, NX), me_x).start()
     incoming[me_x] = outgoing[me_x]
 
+    @pl.loop(1, plane)
+    def _(step):
+        reduce_copy(me_plane, lax.rem(me_plane + step, plane)).wait_recv()
+
+    total = reduced[0].astype(F32)
+    for i in range(1, plane):
+        total = total + reduced[i].astype(F32)
+    gathered[me_side] = total.astype(BF16)
+
+    def side_copy(to, slot):
+        return pltpu.make_async_remote_copy(
+            src_ref=gathered.at[me_side],
+            dst_ref=gathered.at[slot],
+            send_sem=side_send.at[to],
+            recv_sem=side_recv.at[slot],
+            device_id=at_side(to),
+            device_id_type=MESH,
+        )
+
+    @pl.loop(1, side)
+    def _(step):
+        side_copy(lax.rem(me_side + step, side), me_side).start()
+
     @pl.loop(1, side)
     def _(step):
         side_copy(me_side, lax.rem(me_side + step, side)).wait_recv()
@@ -363,7 +361,27 @@
     mask = jnp.where(r == c // BLK, 1.0, 0.0).astype(BF16)
 
     def widen(x):
-        copies[x] = dot(incoming[x], spread).astype(BF16)
+        copies[...] = dot(incoming[x], spread).astype(BF16)
+
+        @pl.loop(0, 8)
+        def _(small):
+            for big in range(4):
+                group = big * 8 + small
+                at = pl.ds(pl.multiple_of(group * 16, 16), 16)
+                for p in range(2):
+                    for w in range(WIN):
+                        quarter = p * 2 + w
+                        tile = copies[at, quarter * 128 : quarter * 128 + 128]
+                        slab = pl.multiple_of((p * 8 + x * 2 + w) * 16, 16)
+                        right[group, pl.ds(slab, 16), :] = (
+                            jnp.concatenate([tile] * 4, axis=1) * mask
+                        )
+
+    widen(me_x)
+    for step in (1, 3, 2):
+        x = lax.rem(me_x + step, NX)
+        white_copy(me_x, x).wait_recv()
+        widen(x)
 
     @pl.loop(0, ny)
     def _(slot):
@@ -382,8 +400,8 @@
         jnp.where(first, jnp.abs(re) + jnp.abs(im), size), axis=1, keepdims=True
     )
     level = WATER * (total / (HALF + 1) + 1e-06)
-    re = re / (jnp.where(first, jnp.abs(re), size) + level)
-    im = im / (jnp.where(first, jnp.abs(im), size) + level)
+    re = (re / (jnp.where(first, jnp.abs(re), size) + level)).astype(BF16)
+    im = (im / (jnp.where(first, jnp.abs(im), size) + level)).astype(BF16)
     parts = []
     for x in range(NX):
         for w in range(WIN):
@@ -404,34 +422,19 @@
                 lax.broadcasted_iota(jnp.int32, shape, 0) < 16,
                 lax.broadcasted_iota(jnp.int32, shape, 1) % 16 == 0,
             )
-            re_b1 = jnp.where(zero_bin, 0.0, re_b1)
-            im_b0 = jnp.where(zero_bin, 0.0, im_b0)
+            zero = jnp.zeros(shape, BF16)
+            re_b1 = jnp.where(zero_bin, zero, re_b1)
+            im_b0 = jnp.where(zero_bin, zero, im_b0)
             im_b1 = jnp.where(zero_bin, a_im, im_b1)
-        left[small, 0, 0] = re_b0.astype(BF16)
-        left[small, 0, 1] = re_b1.astype(BF16)
-        left[small, 1, 0] = im_b0.astype(BF16)
-        left[small, 1, 1] = im_b1.astype(BF16)
-
-    for step in (2, 1, 3):
-        white_copy(me_x, lax.rem(me_x + step, NX)).wait_recv()
-    for x in range(NX):
-        widen(x)
+        left[small, 0, 0] = re_b0
+        left[small, 0, 1] = re_b1
+        left[small, 1, 0] = im_b0
+        left[small, 1, 1] = im_b1
 
     @pl.loop(0, 8)
     def _(small):
         for big in range(4):
             group = big * 8 + small
-            at = pl.ds(pl.multiple_of(group * 16, 16), 16)
-            slabs = []
-            for p in range(2):
-                for x in range(NX):
-                    for w in range(WIN):
-                        quarter = p * 2 + w
-                        tile = copies[x, at, quarter * 128 : quarter * 128 + 128]
-                        slabs.append(
-                            jnp.concatenate([tile] * 4, axis=1) * mask
-                        )
-            right = jnp.concatenate(slabs, axis=0)
             rows_left = jnp.concatenate(
                 [
                     jnp.concatenate(
@@ -442,75 +445,108 @@
                 ],
                 axis=0,
             )
-            result = dot(rows_left, right)
+            result = dot(rows_left, right[group])
             for h in range(4):
                 cross[h, pl.ds(group, 32, stride=32), :] = result[:, 128 * h : 128 * h + 128]
 
-    for part in range(2):
-        for quad in range(4):
-            for h in range(4):
-                parts = [
-                    cross[h, pl.ds((part * 16 + quad * 4 + i) * 32, 32), :] for i in range(4)
-                ]
-                parts = block_transpose(parts)
-                for j in range(4):
-                    at = (part * 16 + h * 4 + j) * 32
-                    stacked[at : at + 32, 128 * quad : 128 * quad + 128] = parts[j].astype(BF16)
-
-    loads[4].wait()
-
-    def z_copy(step, to, slot):
+    loads[3].wait()
+
+    ahead = lax.rem(me_z + 1, NZ)
+    behind = lax.rem(me_z + NZ - 1, NZ)
+    lag_rows = HALF // NZ
+    top = pl.ds(0, lag_rows // 2)
+    bottom = pl.ds(lag_rows // 2, lag_rows // 2)
+
+    def z_copy(chunk, kind, way, to=None):
+        source = [
+            (lags_out.at[chunk, 1, top], lags_out.at[chunk, 1, bottom]),
+            (lags_out.at[chunk, 0, bottom], lags_out.at[chunk, 2, top]),
+            (mixed.at[chunk, 0], mixed.at[chunk, 1]),
+        ][kind][way]
         return pltpu.make_async_remote_copy(
-            src_ref=lags_out.at[step],
-            dst_ref=lags_in.at[slot],
-            send_sem=z_send.at[step],
-            recv_sem=z_recv.at[slot],
-            device_id=at_z(to),
+            src_ref=source,
+            dst_ref=lags_in.at[chunk, kind, way],
+            send_sem=z_send.at[chunk, kind, way],
+            recv_sem=z_recv.at[chunk, kind, way],
+            device_id=at_z((ahead, behind)[way]),
             device_id_type=MESH,
         )
 
-    def lag_block(to):
+    def lag_block(to, chunk):
         at = pl.ds(pl.multiple_of(to * lag_rows, lag_rows), lag_rows)
-        return dot(inverse[at, :], stacked[...])
-
-    z_steps = sorted(range(1, nz), key=lambda step: -min(step, nz - step))
-    for step in z_steps:
-        to = lax.rem(me_z + step, nz)
-        lags_out[step] = lag_block(to).astype(BF16)
-        z_copy(step, to, me_z).start()
-    total = lag_block(me_z)
-    for step in z_steps[::-1]:
-        slot = lax.rem(me_z + step, nz)
-        z_copy(step, me_z, slot).wait_recv()
-        total = total + lags_in[slot].astype(F32)
-    finished[...] = total.astype(BF16)
+        return dot(inverse[at, :], stacked[:, WIDE * chunk : WIDE * chunk + WIDE])
+
+    for chunk in range(CHUNKS):
+        for part in range(2):
+            for quad in range(chunk * 4 // CHUNKS, (chunk + 1) * 4 // CHUNKS):
+                for h in range(4):
+                    parts = [
+                        cross[h, pl.ds((part * 16 + quad * 4 + i) * 32, 32), :].astype(BF16)
+                        for i in range(4)
+                    ]
+                    parts = block_transpose(parts)
+                    for j in range(4):
+                        at = (part * 16 + h * 4 + j) * 32
+                        stacked[at : at + 32, 128 * quad : 128 * quad + 128] = parts[j]
+        lags_out[chunk, 1] = lag_block(lax.rem(me_z + 2, NZ), chunk).astype(BF16)
+        z_copy(chunk, 0, 0).start()
+        z_copy(chunk, 0, 1).start()
+        block = lag_block(ahead, chunk)
+        lags_out[chunk, 0] = block.astype(BF16)
+        kept[chunk, 0] = block[: lag_rows // 2]
+        z_copy(chunk, 1, 0).start()
+        block = lag_block(behind, chunk)
+        lags_out[chunk, 2] = block.astype(BF16)
+        kept[chunk, 1] = block[lag_rows // 2 :]
+        z_copy(chunk, 1, 1).start()
+        block = lag_block(me_z, chunk)
+        kept[chunk, 2] = block[: lag_rows // 2]
+        kept[chunk, 3] = block[lag_rows // 2 :]
+
+    for chunk in range(CHUNKS):
+        for way in range(2):
+            z_copy(chunk, 0, way).wait_recv()
+            total = kept[chunk, way] + lags_in[chunk, 0, way].astype(F32)
+            mixed[chunk, way] = total.astype(BF16)
+            z_copy(chunk, 2, way).start()
 
     own = lag_rows // NX
 
-    def last_copy(to, slot):
+    def last_copy(chunk, to, slot):
         at = pl.ds(pl.multiple_of(to * own, own), own)
         return pltpu.make_async_remote_copy(
-            src_ref=finished.at[at],
-            dst_ref=last.at[slot],
-            send_sem=last_send.at[to],
-            recv_sem=last_recv.at[slot],
+            src_ref=finished.at[chunk, at],
+            dst_ref=last.at[chunk, slot],
+            send_sem=last_send.at[chunk, to],
+            recv_sem=last_recv.at[chunk, slot],
             device_id=at_x(to),
             device_id_type=MESH,
         )
 
-    for step in (2, 1, 3):
-        last_copy(lax.rem(me_x + step, NX), me_x).start()
-    last[me_x] = finished[pl.ds(pl.multiple_of(me_x * own, own), own), :]
-    for step in (1, 3, 2):
-        last_copy(me_x, lax.rem(me_x + step, NX)).wait_recv()
-    for quad in range(4):
-        parts = [
-            last[x, :, 128 * quad : 128 * quad + 128].astype(F32) for x in range(NX)
-        ]
-        parts = block_transpose(parts)
-        for j in range(4):
-            s = quad * 4 + j
-            out[:, 128 * s : 128 * s + 128] = parts[j].astype(BF16)
+    for chunk in range(CHUNKS):
+        for kind in (1, 2):
+            for way in range(2):
+                z_copy(chunk, kind, way).wait_recv()
+        for half in range(2):
+            total = (
+                kept[chunk, 2 + half]
+                + lags_in[chunk, 2, half].astype(F32)
+                + lags_in[chunk, 1, 1 - half].astype(F32)
+            )
+            finished[chunk, pl.ds(half * lag_rows // 2, lag_rows // 2)] = total.astype(BF16)
+        for step in (2, 1, 3):
+            last_copy(chunk, lax.rem(me_x + step, NX), me_x).start()
+        last[chunk, me_x] = finished[chunk, pl.ds(pl.multiple_of(me_x * own, own), own), :]
+
+    for chunk in range(CHUNKS):
+        for step in (1, 3, 2):
+            last_copy(chunk, me_x, lax.rem(me_x + step, NX)).wait_recv()
+        for quad in range(4 // CHUNKS):
+            parts = [last[chunk, x, :, 128 * quad : 128 * quad + 128] for x in range(NX)]
+            parts = block_transpose(parts)
+            for j in range(4):
+                s = chunk * NSRC // CHUNKS + quad * 4 + j
+                out[:, 128 * s : 128 * s + 128] = parts[j]
 
     @pl.loop(1, plane)
     def _(step):
@@ -531,29 +567,32 @@
     for step in (1, 2, 3):
         to = lax.rem(me_x + step, NX)
         white_copy(to, me_x).wait_send()
-        last_copy(to, me_x).wait_send()
-    for step in z_steps:
-        z_copy(step, lax.rem(me_z + step, nz), me_z).wait_send()
-
-
-def local(nchan, nz, record, offsets, sources):
-    lag_rows = HALF // nz
+        for chunk in range(CHUNKS):
+            last_copy(chunk, to, me_x).wait_send()
+    for chunk in range(CHUNKS):
+        for kind in range(3):
+            for way in range(2):
+                z_copy(chunk, kind, way).wait_send()
+
+
+def local(nchan, record, offsets, sources):
+    lag_rows = HALF // NZ
     own = lag_rows // NX
     nlow, ny = split_chan(nchan)
     per = LANES // ny
     upper, lower = forward_tables()
-    inverse = inverse_table(nz * NX * WIN)
+    inverse = inverse_table(NZ * NX * WIN)
+    tables = np.concatenate([upper, lower, inverse], axis=0)
     vmem = pl.BlockSpec(memory_space=pltpu.VMEM)
     hbm = pl.BlockSpec(memory_space=pltpu.HBM)
     dma = pltpu.SemaphoreType.DMA
     flat = pl.pallas_call(
-        functools.partial(kernel, nchan, nz),
+        functools.partial(kernel, nchan),
         out_shape=jax.ShapeDtypeStruct((own, NSRC * ROWS), BF16),
-        in_specs=[hbm, hbm, vmem, hbm, hbm, hbm],
+        in_specs=[hbm, vmem, hbm],
         out_specs=vmem,
         scratch_shapes=[
-            pltpu.SMEM((WIN,), jnp.int32),
-            pltpu.SMEM((NSRC,), jnp.int32),
+            pltpu.SMEM((WIN + NSRC,), jnp.int32),
             pltpu.VMEM((SAMPLES, SAMPLES), BF16),
             pltpu.VMEM((SAMPLES, SAMPLES), BF16),
             pltpu.VMEM((HALF, SAMPLES), BF16),
@@ -567,14 +606,17 @@
             pltpu.VMEM((NX, HALF, 128), BF16),
             pltpu.VMEM((NX, HALF, 128), BF16),
             pltpu.VMEM((8, 2, 2, 64, 128), BF16),
-            pltpu.VMEM((NX, HALF, 512), BF16),
+            pltpu.VMEM((HALF, 512), BF16),
+            pltpu.VMEM((GROUPS, 256, 512), BF16),
             pltpu.VMEM((4, SAMPLES, 128), F32),
             pltpu.VMEM((SAMPLES, 512), BF16),
-            pltpu.VMEM((nz, lag_rows, 512), BF16),
-            pltpu.VMEM((nz, lag_rows, 512), BF16),
-            pltpu.VMEM((lag_rows, 512), BF16),
-            pltpu.VMEM((NX, own, 512), BF16),
-            dma((5,)),
+            pltpu.VMEM((CHUNKS, 3, lag_rows, WIDE), BF16),
+            pltpu.VMEM((CHUNKS, 2, lag_rows // 2, WIDE), BF16),
+            pltpu.VMEM((CHUNKS, 4, lag_rows // 2, WIDE), F32),
+            pltpu.VMEM((CHUNKS, 3, 2, lag_rows // 2, WIDE), BF16),
+            pltpu.VMEM((CHUNKS, lag_rows, WIDE), BF16),
+            pltpu.VMEM((CHUNKS, NX, own, WIDE), BF16),
+            dma((4,)),
             dma((2 * ny,)),
             dma((2 * ny,)),
             dma((nlow * NX,)),
@@ -585,35 +627,31 @@
             dma((ny,)),
             dma((NX,)),
             dma((NX,)),
-            dma((nz,)),
-            dma((nz,)),
-            dma((NX,)),
-            dma((NX,)),
+            dma((CHUNKS, 3, 2)),
+            dma((CHUNKS, 3, 2)),
+            dma((CHUNKS, NX)),
+            dma((CHUNKS, NX)),
         ],
         compiler_params=pltpu.CompilerParams(
-            collective_id=0, has_side_effects=True, vmem_limit_bytes=48 * 1024 * 1024
+            collective_id=0, has_side_effects=True, vmem_limit_bytes=60 * 1024 * 1024
         ),
         cost_estimate=pl.CostEstimate(
             flops=3 * 10**9, bytes_accessed=7 * 10**6, transcendentals=10**6
         ),
     )(
-        offsets,
-        sources,
+        jnp.concatenate([offsets, sources]),
         jnp.transpose(record, (1, 0, 2)),
-        jnp.asarray(upper),
-        jnp.asarray(lower),
-        jnp.asarray(inverse),
+        jnp.asarray(tables),
     )
     return flat.reshape(own, NSRC, ROWS)
 
 
 def solution(mesh):
     nchan = mesh.shape["chan"]
-    nz = mesh.shape["spec"] // NX
     in_specs = (P("chan", "spec", None), P("spec"), P())
     out_specs = P("spec", None, "chan")
     return jax.shard_map(
-        functools.partial(local, nchan, nz),
+        functools.partial(local, nchan),
         mesh=mesh,
         in_specs=in_specs,
         out_specs=out_specs,

time: 68.6 us -> 62.8 us (0.915)
  the two profiles are of different devices: /device:TPU:1 before, /device:TPU:2 now
where the time goes in v2:
time: 62.8 us; the launch traced here: 62.5 us
  Pallas kernels  57.8 us (92%)
  local copies, waits for them, and re-layouts  3.51 us (6%)
  other arithmetic  1.26 us (2%)
    pallas_call x1, Pallas kernels, local(): pl.pallas_call(functools.partial(kernel, nchan), out_shape=jax.ShapeDtype...  57.8 us
    unnamed x2, local copies, waits for them, and re-layouts  3.51 us

profile of v2, /device:TPU:2, one launch (start us, length us, event | category | flops | bytes accessed | tf_op | source)
XLA Modules:
  0.0 62.5 jit_solution(9965997068006200013)
XLA Ops:
  0.0 1.3 %pad_add_fusion.numbers_hbm = s32[18]{0:T(128)} fusion(s32[16]{0:T(128)} %param.6, s32[2]{0:T(128)} %param.5), kind=kLoop, calls=%fused_computation.1 | loop fusion | flops 18 | bytes 144 | tf_op jit(solution)/shard_map/concatenate | solution.py:642
  1.3 1.9 %copy.8 = bf16[128,2,1152]{2,0,1:T(8,128)(2,1)} copy(bf16[128,2,1152]{2,1,0:T(2,128)(2,1)} %param.4) | data formatting | bytes 1179648 | tf_op args[0]
  3.2 57.8 %shard_map.46 = bf16[32,2048]{1,0:T(8,128)(2,1)} custom-call(s32[18]{0:T(128)} %pad_add_fusion.numbers_hbm, bf16[2,128,1152]{2,1,0:T(8,128)(2,1)} %bitcast.5, bf16[2560,1024]{1,0:T(8,128)(2,1)} %constant.2.clone.tables_hbm), custom_call_target="tpu_custom_call" | custom-call | flops 3000000000 | bytes 7000000 | tf_op jit(solution)/shard_map/pallas_call | solution.py:589
  61.0 1.6 %copy.6 = bf16[4,8,16,128]{3,2,1,0:T(8,128)(2,1)} copy(bf16[4,8,16,128]{3,1,2,0:T(8,128)(2,1)} %bitcast.6) | data formatting | bytes 262144

commit v3 on v2

--- a/solution.py
+++ b/solution.py
@@ -19,7 +19,7 @@
 WIN = 2
 BLK = ROWS // NX
 GROUPS = 32
-LANES = SAMPLES // 128
+NLOW = 2
 NZ = 4
 CHUNKS = 2
 WIDE = NSRC * BLK // CHUNKS
@@ -53,11 +53,6 @@
     return table.astype(jnp.bfloat16)
 
 
-def split_chan(nchan):
-    nlow = 2 if nchan >= 8 else 1
-    return nlow, nchan // (2 * nlow)
-
-
 def dot_t(left, right):
     return lax.dot_general(left, right, (((1,), (1,)), ((), ())), preferred_element_type=F32)
 
@@ -86,20 +81,21 @@
 
 
 def kernel(
-    nchan,
-    numbers_hbm,
+    ny,
+    offsets_hbm,
+    sources_hbm,
     record,
     tables_hbm,
     out,
-    numbers,
+    offsets,
+    sources,
     upper,
     lower,
     inverse,
     traces,
     pieces,
     reduced,
-    gathered,
-    piece_out,
+    parts_y,
     picked,
     spectrum,
     outgoing,
@@ -116,12 +112,12 @@
     finished,
     last,
     load_sem,
-    reduce_send,
-    reduce_recv,
+    near_send,
+    near_recv,
+    y_send,
+    y_recv,
     side_send,
     side_recv,
-    y_send,
-    y_recv,
     core_send,
     core_recv,
     white_send,
@@ -131,10 +127,9 @@
     last_send,
     last_recv,
 ):
-    nlow, ny = split_chan(nchan)
-    per = LANES // ny
     plane = 2 * ny
-    side = nlow * NX
+    side = NLOW * NX
+    near = NLOW * 2
     chan = lax.axis_index("chan")
     spec = lax.axis_index("spec")
     me_x = lax.rem(spec, NX)
@@ -144,9 +139,13 @@
     me_y = me_plane // 2
     me_core = lax.rem(chan, 2)
     me_side = me_low * NX + me_x
-
-    def at_plane(other):
-        return (me_low * plane + other, spec)
+    me_near = me_low * 2 + me_core
+
+    def at_near(other):
+        return (other // 2 * plane + me_y * 2 + lax.rem(other, 2), spec)
+
+    def at_y(other):
+        return (me_low * plane + other * 2 + me_core, spec)
 
     def at_side(other):
         return (other // NX * plane + me_plane, me_z * NX + lax.rem(other, NX))
@@ -161,7 +160,8 @@
         pltpu.make_async_copy(source, target, load_sem.at[i])
         for i, (source, target) in enumerate(
             [
-                (numbers_hbm, numbers),
+                (offsets_hbm, offsets),
+                (sources_hbm, sources),
                 (tables_hbm.at[pl.ds(0, SAMPLES)], upper),
                 (tables_hbm.at[pl.ds(SAMPLES, SAMPLES)], lower),
                 (tables_hbm.at[pl.ds(2 * SAMPLES, HALF)], inverse),
@@ -173,29 +173,30 @@
 
     barrier = pltpu.get_barrier_semaphore()
 
-    @pl.loop(1, plane)
+    def greet(device):
+        pl.semaphore_signal(barrier, inc=1, device_id=device, device_id_type=MESH)
+
+    greet(at_near(me_low * 2 + 1 - me_core))
+    greet(at_near((1 - me_low) * 2 + 1 - me_core))
+
+    @pl.loop(1, ny)
     def _(step):
-        pl.semaphore_signal(
-            barrier, inc=1, device_id=at_plane(lax.rem(me_plane + step, plane)), device_id_type=MESH
-        )
+        greet(at_y(lax.rem(me_y + step, ny)))
 
     @pl.loop(1, side)
     def _(step):
-        pl.semaphore_signal(
-            barrier, inc=1, device_id=at_side(lax.rem(me_side + step, side)), device_id_type=MESH
-        )
+        greet(at_side(lax.rem(me_side + step, side)))
 
     for step in (1, NZ - 1):
-        pl.semaphore_signal(
-            barrier, inc=1, device_id=at_z(lax.rem(me_z + step, NZ)), device_id_type=MESH
-        )
+        greet(at_z(lax.rem(me_z + step, NZ)))
 
     loads[0].wait()
+    loads[1].wait()
 
     lane = lax.broadcasted_iota(jnp.int32, (ROWS, 128), 1)
     for w in range(WIN):
         rows = record[w].astype(F32)
-        head = jnp.where(lane < numbers[w], rows[:, SAMPLES:], rows[:, :PAD])
+        head = jnp.where(lane < offsets[w], rows[:, SAMPLES:], rows[:, :PAD])
         rows = jnp.concatenate([head, rows[:, PAD:SAMPLES]], axis=1)
         rows = rows - jnp.mean(rows, axis=1, keepdims=True)
         rows = rows * lax.rsqrt(jnp.mean(rows * rows, axis=1, keepdims=True) + 1e-06)
@@ -207,37 +208,56 @@
     col = lax.broadcasted_iota(jnp.int32, (32, 256), 1)
     wanted = jnp.zeros((32, 256), jnp.int32)
     for s in range(NSRC):
-        wanted = jnp.where(row % NSRC == s, numbers[WIN + s], wanted)
+        wanted = jnp.where(row % NSRC == s, sources[s], wanted)
     channel = chan * ROWS + (col // 64) * BLK + col % BLK
     same = jnp.logical_and(wanted == channel, row // NSRC == (col // BLK) % 2)
     chosen = dot(jnp.where(same, 1.0, 0.0).astype(BF16), traces[...])
-    chosen = chosen.astype(BF16)
     for w in range(WIN):
-        for l in range(LANES):
-            pieces[w, l] = chosen[NSRC * w : NSRC * w + NSRC, 128 * l : 128 * l + 128]
-
-    pl.semaphore_wait(barrier, plane - 1 + side - 1 + 2)
-
-    def reduce_copy(to, slot):
+        for low in range(NLOW):
+            rows = chosen[16 * w + 8 * low : 16 * w + 8 * low + 8]
+            rows = jnp.concatenate([rows[:, :HALF], rows[:, HALF:]], axis=0)
+            pieces[low * 2 + w] = rows.astype(BF16)
+
+    pl.semaphore_wait(barrier, 2 + ny - 1 + side - 1 + 2)
+
+    def near_copy(to, slot):
         return pltpu.make_async_remote_copy(
-            src_ref=pieces.at[lax.rem(to, 2), pl.ds(to // 2 * per, per)],
+            src_ref=pieces.at[to],
             dst_ref=reduced.at[slot],
-            send_sem=reduce_send.at[to],
-            recv_sem=reduce_recv.at[slot],
-            device_id=at_plane(to),
+            send_sem=near_send.at[to],
+            recv_sem=near_recv.at[slot],
+            device_id=at_near(to),
             device_id_type=MESH,
         )
 
-    @pl.loop(1, plane)
-    def _(step):
-        reduce_copy(lax.rem(me_plane + step, plane), me_plane).start()
-
-    reduced[me_plane] = pieces[me_core, pl.ds(me_y * per, per)]
-    loads[1].wait()
+    for step in (2, 3, 1):
+        near_copy(lax.rem(me_near + step, near), me_near).start()
+    reduced[me_near] = pieces[me_near]
     loads[2].wait()
+    loads[3].wait()
 
     spectrum[...] = dot_t(upper[...], traces[...])
     spectrum[...] += dot_t(lower[...], traces[...])
+
+    for step in (1, 2, 3):
+        near_copy(me_near, lax.rem(me_near + step, near)).wait_recv()
+    total = reduced[0].astype(F32)
+    for i in range(1, near):
+        total = total + reduced[i].astype(F32)
+    parts_y[me_y] = total.astype(BF16)
+
+    def y_copy(to, slot):
+        return pltpu.make_async_remote_copy(
+            src_ref=parts_y.at[me_y],
+            dst_ref=parts_y.at[slot],
+            send_sem=y_send.at[to],
+            recv_sem=y_recv.at[slot],
+            device_id=at_y(to),
+            device_id_type=MESH,
+        )
+
+    for step in sorted(range(1, ny), key=lambda step: -min(step, ny - step)):
+        y_copy(lax.rem(me_y + step, ny), me_y).start()
 
     chunk = 64
     first_row = lax.broadcasted_iota(jnp.int32, (chunk, 256), 0) == 0
@@ -284,74 +304,6 @@
         white_copy(lax.rem(me_x + step, NX), me_x).start()
     incoming[me_x] = outgoing[me_x]
 
-    @pl.loop(1, plane)
-    def _(step):
-        reduce_copy(me_plane, lax.rem(me_plane + step, plane)).wait_recv()
-
-    total = reduced[0].astype(F32)
-    for i in range(1, plane):
-        total = total + reduced[i].astype(F32)
-    gathered[me_side] = total.astype(BF16)
-
-    def side_copy(to, slot):
-        return pltpu.make_async_remote_copy(
-            src_ref=gathered.at[me_side],
-            dst_ref=gathered.at[slot],
-            send_sem=side_send.at[to],
-            recv_sem=side_recv.at[slot],
-            device_id=at_side(to),
-            device_id_type=MESH,
-        )
-
-    @pl.loop(1, side)
-    def _(step):
-        side_copy(lax.rem(me_side + step, side), me_side).start()
-
-    @pl.loop(1, side)
-    def _(step):
-        side_copy(me_side, lax.rem(me_side + step, side)).wait_recv()
-
-    for l in range(per):
-        for x in range(NX):
-            total = gathered[x, l].astype(F32)
-            for low_z in range(1, nlow):
-                total = total + gathered[low_z * NX + x, l].astype(F32)
-            piece_out[l, NSRC * x : NSRC * x + NSRC] = total.astype(BF16)
-
-    def y_copy(to, slot):
-        return pltpu.make_async_remote_copy(
-            src_ref=piece_out,
-            dst_ref=picked.at[me_core, pl.ds(slot * per, per)],
-            send_sem=y_send.at[to],
-            recv_sem=y_recv.at[slot],
-            device_id=at_plane(to * 2 + me_core),
-            device_id_type=MESH,
-        )
-
-    def core_copy(core, slot):
-        at = picked.at[core, pl.ds(slot * per, per)]
-        return pltpu.make_async_remote_copy(
-            src_ref=at,
-            dst_ref=at,
-            send_sem=core_send.at[slot],
-            recv_sem=core_recv.at[slot],
-            device_id=at_plane(me_y * 2 + 1 - me_core),
-            device_id_type=MESH,
-        )
-
-    @pl.loop(1, ny)
-    def _(step):
-        y_copy(lax.rem(me_y + step, ny), me_y).start()
-
-    picked[me_core, pl.ds(me_y * per, per)] = piece_out[...]
-    core_copy(me_core, me_y).start()
-
-    @pl.loop(1, ny)
-    def _(step):
-        slot = lax.rem(me_y + step, ny)
-        y_copy(me_y, slot).wait_recv()
-        core_copy(me_core, slot).start()
-
     r = lax.broadcasted_iota(jnp.int32, (128, 512), 0)
     c = lax.broadcasted_iota(jnp.int32, (128, 512), 1)
     match = jnp.logical_and(r // BLK == c // 128, r % BLK == c % BLK)
@@ -377,44 +329,85 @@
                             jnp.concatenate([tile] * 4, axis=1) * mask
                         )
 
+    @pl.loop(1, ny)
+    def _(step):
+        y_copy(me_y, lax.rem(me_y + step, ny)).wait_recv()
+
+    total = parts_y[0].astype(F32)
+    for i in range(1, ny):
+        total = total + parts_y[i].astype(F32)
+    rows = jnp.concatenate([total[:8], total[8:]], axis=1).astype(BF16)
+    both = dot_t(rows, upper[...]) + dot_t(rows, lower[...])
+    re = both[:, :HALF]
+    im = both[:, HALF:]
+    size = jnp.sqrt(re * re + im * im)
+    first = lax.broadcasted_iota(jnp.int32, (8, HALF), 1) == 0
+    total = jnp.sum(
+        jnp.where(first, jnp.abs(re) + jnp.abs(im), size), axis=1, keepdims=True
+    )
+    level = WATER * (total / (HALF + 1) + 1e-06)
+    re = re / (jnp.where(first, jnp.abs(re), size) + level)
+    im = im / (jnp.where(first, jnp.abs(im), size) + level)
+    picked[me_core, me_side] = jnp.concatenate([re, im], axis=0).astype(BF16)
+
+    def side_copy(to, slot):
+        return pltpu.make_async_remote_copy(
+            src_ref=picked.at[me_core, me_side],
+            dst_ref=picked.at[me_core, slot],
+            send_sem=side_send.at[to],
+            recv_sem=side_recv.at[slot],
+            device_id=at_side(to),
+            device_id_type=MESH,
+        )
+
+    def core_copy(core, slot):
+        return pltpu.make_async_remote_copy(
+            src_ref=picked.at[core, slot],
+            dst_ref=picked.at[core, slot],
+            send_sem=core_send.at[slot],
+            recv_sem=core_recv.at[slot],
+            device_id=at_near(me_low * 2 + 1 - me_core),
+            device_id_type=MESH,
+        )
+
+    @pl.loop(1, side)
+    def _(step):
+        side_copy(lax.rem(me_side + step, side), me_side).start()
+
+    core_copy(me_core, me_side).start()
+
     widen(me_x)
     for step in (1, 3, 2):
         x = lax.rem(me_x + step, NX)
         white_copy(me_x, x).wait_recv()
         widen(x)
 
-    @pl.loop(0, ny)
+    @pl.loop(1, side)
+    def _(step):
+        slot = lax.rem(me_side + step, side)
+        side_copy(me_side, slot).wait_recv()
+        core_copy(me_core, slot).start()
+
+    @pl.loop(0, side)
     def _(slot):
         core_copy(1 - me_core, slot).wait_recv()
 
-    rows = [
-        jnp.concatenate([picked[w, l] for l in range(LANES)], axis=1) for w in range(WIN)
-    ]
-    rows = jnp.concatenate(rows, axis=0)
-    both = dot_t(rows, upper[...]) + dot_t(rows, lower[...])
-    re = both[:, :HALF]
-    im = both[:, HALF:]
-    size = jnp.sqrt(re * re + im * im)
-    first = lax.broadcasted_iota(jnp.int32, (ROWS, HALF), 1) == 0
-    total = jnp.sum(
-        jnp.where(first, jnp.abs(re) + jnp.abs(im), size), axis=1, keepdims=True
-    )
-    level = WATER * (total / (HALF + 1) + 1e-06)
-    re = (re / (jnp.where(first, jnp.abs(re), size) + level)).astype(BF16)
-    im = (im / (jnp.where(first, jnp.abs(im), size) + level)).astype(BF16)
     parts = []
     for x in range(NX):
         for w in range(WIN):
             tiles = []
-            for half in (re, im):
+            halves = [picked[w, low * NX + x].astype(F32) for low in range(NLOW)]
+            for part in range(2):
                 for big in range(4):
-                    at = NSRC * (w * NX + x)
-                    tiles.append(half[at : at + NSRC, 128 * big : 128 * big + 128])
+                    for half in halves:
+                        tiles.append(
+                            half[8 * part : 8 * part + 8, 128 * big : 128 * big + 128]
+                        )
             parts.append(jnp.concatenate(tiles, axis=0))
     parts = block_transpose(parts)
     for small in range(8):
-        a_re = parts[small][:64]
-        a_im = parts[small][64:]
+        a_re = parts[small][:64].astype(BF16)
+        a_im = parts[small][64:].astype(BF16)
         re_b0, re_b1, im_b0, im_b1 = a_re, a_im, -a_im, a_re
         if small == 0:
             shape = (64, 128)
@@ -449,7 +442,7 @@
             for h in range(4):
                 cross[h, pl.ds(group, 32, stride=32), :] = result[:, 128 * h : 128 * h + 128]
 
-    loads[3].wait()
+    loads[4].wait()
 
     ahead = lax.rem(me_z + 1, NZ)
     behind = lax.rem(me_z + NZ - 1, NZ)
@@ -548,19 +541,18 @@
                 s = chunk * NSRC // CHUNKS + quad * 4 + j
                 out[:, 128 * s : 128 * s + 128] = parts[j]
 
-    @pl.loop(1, plane)
+    for step in (1, 2, 3):
+        near_copy(lax.rem(me_near + step, near), me_near).wait_send()
+
+    @pl.loop(1, ny)
     def _(step):
-        reduce_copy(lax.rem(me_plane + step, plane), me_plane).wait_send()
+        y_copy(lax.rem(me_y + step, ny), me_y).wait_send()
 
     @pl.loop(1, side)
     def _(step):
         side_copy(lax.rem(me_side + step, side), me_side).wait_send()
 
-    @pl.loop(1, ny)
-    def _(step):
-        y_copy(lax.rem(me_y + step, ny), me_y).wait_send()
-
-    @pl.loop(0, ny)
+    @pl.loop(0, side)
     def _(slot):
         core_copy(me_core, slot).wait_send()
 
@@ -575,11 +567,9 @@
                 z_copy(chunk, kind, way).wait_send()
 
 
-def local(nchan, record, offsets, sources):
+def local(ny, record, offsets, sources):
     lag_rows = HALF // NZ
     own = lag_rows // NX
-    nlow, ny = split_chan(nchan)
-    per = LANES // ny
     upper, lower = forward_tables()
     inverse = inverse_table(NZ * NX * WIN)
     tables = np.concatenate([upper, lower, inverse], axis=0)
@@ -587,21 +577,21 @@
     hbm = pl.BlockSpec(memory_space=pltpu.HBM)
     dma = pltpu.SemaphoreType.DMA
     flat = pl.pallas_call(
-        functools.partial(kernel, nchan),
+        functools.partial(kernel, ny),
         out_shape=jax.ShapeDtypeStruct((own, NSRC * ROWS), BF16),
-        in_specs=[hbm, vmem, hbm],
+        in_specs=[hbm, hbm, vmem, hbm],
         out_specs=vmem,
         scratch_shapes=[
-            pltpu.SMEM((WIN + NSRC,), jnp.int32),
+            pltpu.SMEM((WIN,), jnp.int32),
+            pltpu.SMEM((NSRC,), jnp.int32),
             pltpu.VMEM((SAMPLES, SAMPLES), BF16),
             pltpu.VMEM((SAMPLES, SAMPLES), BF16),
             pltpu.VMEM((HALF, SAMPLES), BF16),
             pltpu.VMEM((256, SAMPLES), BF16),
-            pltpu.VMEM((WIN, LANES, NSRC, 128), BF16),
-            pltpu.VMEM((2 * ny, per, NSRC, 128), BF16),
-            pltpu.VMEM((nlow * NX, per, NSRC, 128), BF16),
-            pltpu.VMEM((per, NX * NSRC, 128), BF16),
-            pltpu.VMEM((WIN, LANES, NX * NSRC, 128), BF16),
+            pltpu.VMEM((2 * NLOW, 16, HALF), BF16),
+            pltpu.VMEM((2 * NLOW, 16, HALF), BF16),
+            pltpu.VMEM((ny, 16, HALF), BF16),
+            pltpu.VMEM((2, NLOW * NX, 16, HALF), BF16),
             pltpu.VMEM((SAMPLES, 256), F32),
             pltpu.VMEM((NX, HALF, 128), BF16),
             pltpu.VMEM((NX, HALF, 128), BF16),
@@ -616,15 +606,15 @@
             pltpu.VMEM((CHUNKS, 3, 2, lag_rows // 2, WIDE), BF16),
             pltpu.VMEM((CHUNKS, lag_rows, WIDE), BF16),
             pltpu.VMEM((CHUNKS, NX, own, WIDE), BF16),
-            dma((4,)),
-            dma((2 * ny,)),
-            dma((2 * ny,)),
-            dma((nlow * NX,)),
-            dma((nlow * NX,)),
+            dma((5,)),
+            dma((2 * NLOW,)),
+            dma((2 * NLOW,)),
             dma((ny,)),
             dma((ny,)),
-            dma((ny,)),
-            dma((ny,)),
+            dma((NLOW * NX,)),
+            dma((NLOW * NX,)),
+            dma((NLOW * NX,)),
+            dma((NLOW * NX,)),
             dma((NX,)),
             dma((NX,)),
             dma((CHUNKS, 3, 2)),
@@ -639,7 +629,8 @@
             flops=3 * 10**9, bytes_accessed=7 * 10**6, transcendentals=10**6
         ),
     )(
-        jnp.concatenate([offsets, sources]),
+        offsets,
+        sources,
         jnp.transpose(record, (1, 0, 2)),
         jnp.asarray(tables),
     )
@@ -647,11 +638,11 @@
 
 
 def solution(mesh):
-    nchan = mesh.shape["chan"]
+    ny = mesh.shape["chan"] // (2 * NLOW)
     in_specs = (P("chan", "spec", None), P("spec"), P())
     out_specs = P("spec", None, "chan")
     return jax.shard_map(
-        functools.partial(local, nchan),
+        functools.partial(local, ny),
         mesh=mesh,
         in_specs=in_specs,
         out_specs=out_specs,

time: 62.8 us -> 56.8 us (0.904)
  the two profiles are of different devices: /device:TPU:2 before, /device:TPU:1 now
where the time goes in v3:
time: 56.8 us; the launch traced here: 56.6 us
  Pallas kernels  53.1 us (93%)
  local copies, waits for them, and re-layouts  3.51 us (6%)
    pallas_call x1, Pallas kernels, local(): pl.pallas_call(functools.partial(kernel, ny), out_shape=jax.ShapeDtypeStr...  53.1 us
    unnamed x2, local copies, waits for them, and re-layouts  3.51 us

profile of v3, /device:TPU:1, one launch (start us, length us, event | category | flops | bytes accessed | tf_op | source)
XLA Modules:
  0.0 56.6 jit_solution(10660781359865152796)
XLA Ops:
  0.0 1.9 %copy.8 = bf16[128,2,1152]{2,0,1:T(8,128)(2,1)} copy(bf16[128,2,1152]{2,1,0:T(2,128)(2,1)} %param.4) | data formatting | bytes 1179648 | tf_op args[0]
  1.9 53.1 %shard_map.46 = bf16[32,2048]{1,0:T(8,128)(2,1)} custom-call(s32[2]{0:T(128)} %offsets_hbm.1, s32[16]{0:T(128)} %sources_hbm.1, bf16[2,128,1152]{2,1,0:T(8,128)(2,1)} %bitcast.5, bf16[2560,1024]{1,0:T(8,128)(2,1)} %constant.2.clone.tables_hbm), custom_call_target="tpu_custom_call" | custom-call | flops 3000000000 | bytes 7000000 | tf_op jit(solution)/shard_map/pallas_call | solution.py:579
  55.0 1.6 %copy.6 = bf16[4,8,16,128]{3,2,1,0:T(8,128)(2,1)} copy(bf16[4,8,16,128]{3,1,2,0:T(8,128)(2,1)} %bitcast.6) | data formatting | bytes 262144

commit v4 on v3

--- a/solution.py
+++ b/solution.py
@@ -329,6 +329,8 @@
                             jnp.concatenate([tile] * 4, axis=1) * mask
                         )
 
+    widen(me_x)
+
     @pl.loop(1, ny)
     def _(step):
         y_copy(me_y, lax.rem(me_y + step, ny)).wait_recv()
@@ -376,17 +378,21 @@
 
     core_copy(me_core, me_side).start()
 
-    widen(me_x)
-    for step in (1, 3, 2):
+    def widen_next(step):
         x = lax.rem(me_x + step, NX)
         white_copy(me_x, x).wait_recv()
         widen(x)
+
+    widen_next(1)
+    widen_next(3)
 
     @pl.loop(1, side)
     def _(step):
         slot = lax.rem(me_side + step, side)
         side_copy(me_side, slot).wait_recv()
         core_copy(me_core, slot).start()
+
+    widen_next(2)
 
     @pl.loop(0, side)
     def _(slot):
@@ -623,7 +629,7 @@
             dma((CHUNKS, NX)),
         ],
         compiler_params=pltpu.CompilerParams(
-            collective_id=0, has_side_effects=True, vmem_limit_bytes=60 * 1024 * 1024
+            collective_id=0, has_side_effects=True, vmem_limit_bytes=53 * 1024 * 1024
         ),
         cost_estimate=pl.CostEstimate(
             flops=3 * 10**9, bytes_accessed=7 * 10**6, transcendentals=10**6

time: 56.8 us -> 54.8 us (0.965)
  Pallas kernels: 53.1 us -> 51.5 us
    pallas_call x1, Pallas kernels: 53.1 us -> 51.5 us  [local(): pl.pallas_call(functools.partial(kernel, ny), out_shape=jax.ShapeDtypeStr...]
    unnamed x2 -> x6, local copies, waits for them, and re-layouts: 3.51 us -> 3.11 us
where the time goes in v4:
time: 54.8 us; the launch traced here: 54.6 us
  Pallas kernels  51.5 us (94%)
  local copies, waits for them, and re-layouts  3.11 us (6%)
    pallas_call x1, Pallas kernels, local(): pl.pallas_call(functools.partial(kernel, ny), out_shape=jax.ShapeDtypeStr...  51.5 us
    unnamed x6, local copies, waits for them, and re-layouts  3.11 us

profile of v4, /device:TPU:1, one launch (start us, length us, event | category | flops | bytes accessed | tf_op | source)
XLA Modules:
  0.0 54.6 jit_solution(16156121221371283157)
XLA Ops:
  0.0 1.1 %copy.8 = bf16[128,2,1152]{2,0,1:T(8,128)(2,1)S(1)} copy(bf16[128,2,1152]{2,1,0:T(2,128)(2,1)} %param.4) | data formatting | bytes 1179648 | tf_op args[0]
  1.1 0.0 copy-start
  1.1 0.6 %copy-done = s32[2]{0:T(128)S(1)} copy-done((s32[2]{0:T(128)S(1)}, s32[2]{0:T(128)}, u32[]{:S(2)}) %copy-start) | copy-done | bytes 32
  1.8 0.0 copy-start.1
  1.8 0.7 %copy-done.1 = s32[16]{0:T(128)S(1)} copy-done((s32[16]{0:T(128)S(1)}, s32[16]{0:T(128)}, u32[]{:S(2)}) %copy-start.1) | copy-done | bytes 88
  2.4 51.5 %shard_map.46 = bf16[32,2048]{1,0:T(8,128)(2,1)S(1)} custom-call(s32[2]{0:T(128)S(1)} %copy-done, s32[16]{0:T(128)S(1)} %copy-done.1, bf16[2,128,1152]{2,1,0:T(8,128)(2,1)S(1)} %bitcast.5, bf16[2560,1024]{1,0:T(8,128)(2,1)} %constant.2.clone.tables_hbm), custom_call_target="tpu_custom_call" | custom-call | flops 3000000000 | bytes 7000000 | tf_op jit(solution)/shard_map/pallas_call | solution.py:585
  54.0 0.7 %copy.6 = bf16[4,8,16,128]{3,2,1,0:T(8,128)(2,1)} copy(bf16[4,8,16,128]{3,1,2,0:T(8,128)(2,1)S(1)} %bitcast.6) | data formatting | bytes 262144
Async XLA Ops:
  1.1 0.7 %copy-start = (s32[2]{0:T(128)S(1)}, s32[2]{0:T(128)}, u32[]{:S(2)}) copy-start(s32[2]{0:T(128)} %offsets_hbm.1) | copy-start | bytes 28
  1.8 0.7 %copy-start.1 = (s32[16]{0:T(128)S(1)}, s32[16]{0:T(128)}, u32[]{:S(2)}) copy-start(s32[16]{0:T(128)} %sources_hbm.1) | copy-start | bytes 196

commit v5 on v4

--- a/solution.py
+++ b/solution.py
@@ -22,7 +22,8 @@
 NLOW = 2
 NZ = 4
 CHUNKS = 2
-WIDE = NSRC * BLK // CHUNKS
+PART = BLK // CHUNKS
+WIDE = NSRC * PART
 F32 = jnp.float32
 BF16 = jnp.bfloat16
 MESH = pl.DeviceIdType.MESH
@@ -118,8 +119,6 @@
     y_recv,
     side_send,
     side_recv,
-    core_send,
-    core_recv,
     white_send,
     white_recv,
     z_send,
@@ -128,7 +127,6 @@
     last_recv,
 ):
     plane = 2 * ny
-    side = NLOW * NX
     near = NLOW * 2
     chan = lax.axis_index("chan")
     spec = lax.axis_index("spec")
@@ -147,8 +145,23 @@
     def at_y(other):
         return (me_low * plane + other * 2 + me_core, spec)
 
-    def at_side(other):
-        return (other // NX * plane + me_plane, me_z * NX + lax.rem(other, NX))
+    around = sorted(
+        (
+            (low, x, core)
+            for low in range(NLOW)
+            for x in range(NX)
+            for core in range(2)
+            if low + x + core
+        ),
+        key=lambda step: -(step[0] + 2 * min(step[1], NX - step[1])),
+    )
+
+    def moved(step):
+        low = lax.rem(me_low + step[0], NLOW)
+        x = lax.rem(me_x + step[1], NX)
+        core = lax.rem(me_core + step[2], 2)
+        device = (low * plane + me_y * 2 + core, me_z * NX + x)
+        return device, core, low * NX + x
 
     def at_x(other):
         return (chan, me_z * NX + other)
@@ -176,16 +189,12 @@
     def greet(device):
         pl.semaphore_signal(barrier, inc=1, device_id=device, device_id_type=MESH)
 
-    greet(at_near(me_low * 2 + 1 - me_core))
-    greet(at_near((1 - me_low) * 2 + 1 - me_core))
-
     @pl.loop(1, ny)
     def _(step):
         greet(at_y(lax.rem(me_y + step, ny)))
 
-    @pl.loop(1, side)
-    def _(step):
-        greet(at_side(lax.rem(me_side + step, side)))
+    for step in around:
+        greet(moved(step)[0])
 
     for step in (1, NZ - 1):
         greet(at_z(lax.rem(me_z + step, NZ)))
@@ -218,7 +227,7 @@
             rows = jnp.concatenate([rows[:, :HALF], rows[:, HALF:]], axis=0)
             pieces[low * 2 + w] = rows.astype(BF16)
 
-    pl.semaphore_wait(barrier, 2 + ny - 1 + side - 1 + 2)
+    pl.semaphore_wait(barrier, ny - 1 + len(around) + 2)
 
     def near_copy(to, slot):
         return pltpu.make_async_remote_copy(
@@ -234,10 +243,7 @@
         near_copy(lax.rem(me_near + step, near), me_near).start()
     reduced[me_near] = pieces[me_near]
     loads[2].wait()
-    loads[3].wait()
-
     spectrum[...] = dot_t(upper[...], traces[...])
-    spectrum[...] += dot_t(lower[...], traces[...])
 
     for step in (1, 2, 3):
         near_copy(me_near, lax.rem(me_near + step, near)).wait_recv()
@@ -258,6 +264,9 @@
 
     for step in sorted(range(1, ny), key=lambda step: -min(step, ny - step)):
         y_copy(lax.rem(me_y + step, ny), me_y).start()
+
+    loads[3].wait()
+    spectrum[...] += dot_t(lower[...], traces[...])
 
     chunk = 64
     first_row = lax.broadcasted_iota(jnp.int32, (chunk, 256), 0) == 0
@@ -304,13 +313,14 @@
         white_copy(lax.rem(me_x + step, NX), me_x).start()
     incoming[me_x] = outgoing[me_x]
 
-    r = lax.broadcasted_iota(jnp.int32, (128, 512), 0)
-    c = lax.broadcasted_iota(jnp.int32, (128, 512), 1)
-    match = jnp.logical_and(r // BLK == c // 128, r % BLK == c % BLK)
+    r = lax.broadcasted_iota(jnp.int32, (128, 1024), 0)
+    c = lax.broadcasted_iota(jnp.int32, (128, 1024), 1)
+    match = jnp.logical_and(r // BLK == c // 256, r % BLK // PART == c // 128 % 2)
+    match = jnp.logical_and(match, r % PART == c % PART)
     spread = jnp.where(match, 1.0, 0.0).astype(BF16)
-    r = lax.broadcasted_iota(jnp.int32, (16, 512), 0)
-    c = lax.broadcasted_iota(jnp.int32, (16, 512), 1)
-    mask = jnp.where(r == c // BLK, 1.0, 0.0).astype(BF16)
+    r = lax.broadcasted_iota(jnp.int32, (16, 256), 0)
+    c = lax.broadcasted_iota(jnp.int32, (16, 256), 1)
+    mask = jnp.where(r == c // PART, 1.0, 0.0).astype(BF16)
 
     def widen(x):
         copies[...] = dot(incoming[x], spread).astype(BF16)
@@ -322,12 +332,13 @@
                 at = pl.ds(pl.multiple_of(group * 16, 16), 16)
                 for p in range(2):
                     for w in range(WIN):
-                        quarter = p * 2 + w
-                        tile = copies[at, quarter * 128 : quarter * 128 + 128]
                         slab = pl.multiple_of((p * 8 + x * 2 + w) * 16, 16)
-                        right[group, pl.ds(slab, 16), :] = (
-                            jnp.concatenate([tile] * 4, axis=1) * mask
-                        )
+                        for chunk in range(CHUNKS):
+                            lane = (p * 2 + w) * 256 + chunk * 128
+                            tile = copies[at, lane : lane + 128]
+                            right[chunk, group, pl.ds(slab, 16), :] = (
+                                jnp.concatenate([tile] * 2, axis=1) * mask
+                            )
 
     widen(me_x)
 
@@ -352,31 +363,20 @@
     im = im / (jnp.where(first, jnp.abs(im), size) + level)
     picked[me_core, me_side] = jnp.concatenate([re, im], axis=0).astype(BF16)
 
-    def side_copy(to, slot):
+    def side_copy(step, back=False):
+        device, core, slot = moved(step)
+        at = (core, slot) if back else (me_core, me_side)
         return pltpu.make_async_remote_copy(
             src_ref=picked.at[me_core, me_side],
-            dst_ref=picked.at[me_core, slot],
-            send_sem=side_send.at[to],
-            recv_sem=side_recv.at[slot],
-            device_id=at_side(to),
+            dst_ref=picked.at[at],
+            send_sem=side_send.at[core, slot],
+            recv_sem=side_recv.at[at],
+            device_id=device,
             device_id_type=MESH,
         )
 
-    def core_copy(core, slot):
-        return pltpu.make_async_remote_copy(
-            src_ref=picked.at[core, slot],
-            dst_ref=picked.at[core, slot],
-            send_sem=core_send.at[slot],
-            recv_sem=core_recv.at[slot],
-            device_id=at_near(me_low * 2 + 1 - me_core),
-            device_id_type=MESH,
-        )
-
-    @pl.loop(1, side)
-    def _(step):
-        side_copy(lax.rem(me_side + step, side), me_side).start()
-
-    core_copy(me_core, me_side).start()
+    for step in around:
+        side_copy(step).start()
 
     def widen_next(step):
         x = lax.rem(me_x + step, NX)
@@ -386,17 +386,10 @@
     widen_next(1)
     widen_next(3)
 
-    @pl.loop(1, side)
-    def _(step):
-        slot = lax.rem(me_side + step, side)
-        side_copy(me_side, slot).wait_recv()
-        core_copy(me_core, slot).start()
-
     widen_next(2)
 
-    @pl.loop(0, side)
-    def _(slot):
-        core_copy(1 - me_core, slot).wait_recv()
+    for step in around[::-1]:
+        side_copy(step, True).wait_recv()
 
     parts = []
     for x in range(NX):
@@ -430,23 +423,26 @@
         left[small, 1, 0] = im_b0
         left[small, 1, 1] = im_b1
 
-    @pl.loop(0, 8)
-    def _(small):
-        for big in range(4):
-            group = big * 8 + small
-            rows_left = jnp.concatenate(
-                [
-                    jnp.concatenate(
-                        [left[small, part, p, big * 16 : big * 16 + 16, :] for p in range(2)],
-                        axis=1,
-                    )
-                    for part in range(2)
-                ],
-                axis=0,
-            )
-            result = dot(rows_left, right[group])
-            for h in range(4):
-                cross[h, pl.ds(group, 32, stride=32), :] = result[:, 128 * h : 128 * h + 128]
+    def cross_spectra(chunk):
+        @pl.loop(0, 8)
+        def _(small):
+            for big in range(4):
+                group = big * 8 + small
+                rows_left = jnp.concatenate(
+                    [
+                        jnp.concatenate(
+                            [left[small, part, p, big * 16 : big * 16 + 16, :] for p in range(2)],
+                            axis=1,
+                        )
+                        for part in range(2)
+                    ],
+                    axis=0,
+                )
+                result = dot(rows_left, right[chunk, group])
+                for h in range(2):
+                    cross[chunk, h, pl.ds(group, 32, stride=32), :] = result[
+                        :, 128 * h : 128 * h + 128
+                    ]
 
     loads[4].wait()
 
@@ -476,17 +472,19 @@
         return dot(inverse[at, :], stacked[:, WIDE * chunk : WIDE * chunk + WIDE])
 
     for chunk in range(CHUNKS):
+        cross_spectra(chunk)
         for part in range(2):
-            for quad in range(chunk * 4 // CHUNKS, (chunk + 1) * 4 // CHUNKS):
-                for h in range(4):
+            for octet in range(2):
+                for h in range(2):
                     parts = [
-                        cross[h, pl.ds((part * 16 + quad * 4 + i) * 32, 32), :].astype(BF16)
-                        for i in range(4)
+                        cross[chunk, h, pl.ds((part * 16 + octet * 8 + i) * 32, 32), :].astype(BF16)
+                        for i in range(8)
                     ]
                     parts = block_transpose(parts)
-                    for j in range(4):
-                        at = (part * 16 + h * 4 + j) * 32
-                        stacked[at : at + 32, 128 * quad : 128 * quad + 128] = parts[j]
+                    lane = WIDE * chunk + 128 * octet
+                    for j in range(8):
+                        at = (part * 16 + h * 8 + j) * 32
+                        stacked[at : at + 32, lane : lane + 128] = parts[j]
         lags_out[chunk, 1] = lag_block(lax.rem(me_z + 2, NZ), chunk).astype(BF16)
         z_copy(chunk, 0, 0).start()
         z_copy(chunk, 0, 1).start()
@@ -540,12 +538,16 @@
     for chunk in range(CHUNKS):
         for step in (1, 3, 2):
             last_copy(chunk, me_x, lax.rem(me_x + step, NX)).wait_recv()
-        for quad in range(4 // CHUNKS):
-            parts = [last[chunk, x, :, 128 * quad : 128 * quad + 128] for x in range(NX)]
-            parts = block_transpose(parts)
-            for j in range(4):
-                s = chunk * NSRC // CHUNKS + quad * 4 + j
-                out[:, 128 * s : 128 * s + 128] = parts[j]
+    for octet in range(2):
+        parts = [
+            last[chunk, x, :, 128 * octet : 128 * octet + 128]
+            for x in range(NX)
+            for chunk in range(CHUNKS)
+        ]
+        parts = block_transpose(parts)
+        for j in range(8):
+            s = octet * 8 + j
+            out[:, 128 * s : 128 * s + 128] = parts[j]
 
     for step in (1, 2, 3):
         near_copy(lax.rem(me_near + step, near), me_near).wait_send()
@@ -554,13 +556,8 @@
     def _(step):
         y_copy(lax.rem(me_y + step, ny), me_y).wait_send()
 
-    @pl.loop(1, side)
-    def _(step):
-        side_copy(lax.rem(me_side + step, side), me_side).wait_send()
-
-    @pl.loop(0, side)
-    def _(slot):
-        core_copy(me_core, slot).wait_send()
+    for step in around:
+        side_copy(step).wait_send()
 
     for step in (1, 2, 3):
         to = lax.rem(me_x + step, NX)
@@ -602,9 +599,9 @@
             pltpu.VMEM((NX, HALF, 128), BF16),
             pltpu.VMEM((NX, HALF, 128), BF16),
             pltpu.VMEM((8, 2, 2, 64, 128), BF16),
-            pltpu.VMEM((HALF, 512), BF16),
-            pltpu.VMEM((GROUPS, 256, 512), BF16),
-            pltpu.VMEM((4, SAMPLES, 128), F32),
+            pltpu.VMEM((HALF, 1024), BF16),
+            pltpu.VMEM((CHUNKS, GROUPS, 256, 256), BF16),
+            pltpu.VMEM((CHUNKS, 2, SAMPLES, 128), F32),
             pltpu.VMEM((SAMPLES, 512), BF16),
             pltpu.VMEM((CHUNKS, 3, lag_rows, WIDE), BF16),
             pltpu.VMEM((CHUNKS, 2, lag_rows // 2, WIDE), BF16),
@@ -617,10 +614,8 @@
             dma((2 * NLOW,)),
             dma((ny,)),
             dma((ny,)),
-            dma((NLOW * NX,)),
-            dma((NLOW * NX,)),
-            dma((NLOW * NX,)),
-            dma((NLOW * NX,)),
+            dma((2, NLOW * NX)),
+            dma((2, NLOW * NX)),
             dma((NX,)),
             dma((NX,)),
             dma((CHUNKS, 3, 2)),

time: 54.8 us -> 52.4 us (0.956)
  Pallas kernels: 51.5 us -> 49.1 us
    pallas_call x1, Pallas kernels: 51.5 us -> 49.1 us  [local(): pl.pallas_call(functools.partial(kernel, ny), out_shape=jax.ShapeDtypeStr...]
where the time goes in v5:
time: 52.4 us; the launch traced here: 52.2 us
  Pallas kernels  49.1 us (94%)
  local copies, waits for them, and re-layouts  3.11 us (6%)
    pallas_call x1, Pallas kernels, local(): pl.pallas_call(functools.partial(kernel, ny), out_shape=jax.ShapeDtypeStr...  49.1 us
    unnamed x6, local copies, waits for them, and re-layouts  3.11 us

profile of v5, /device:TPU:1, one launch (start us, length us, event | category | flops | bytes accessed | tf_op | source)
XLA Modules:
  0.0 52.2 jit_solution(6758140160992071812)
XLA Ops:
  0.0 1.1 %copy.8 = bf16[128,2,1152]{2,0,1:T(8,128)(2,1)S(1)} copy(bf16[128,2,1152]{2,1,0:T(2,128)(2,1)} %param.4) | data formatting | bytes 1179648 | tf_op args[0]
  1.1 0.0 copy-start
  1.1 0.6 %copy-done = s32[2]{0:T(128)S(1)} copy-done((s32[2]{0:T(128)S(1)}, s32[2]{0:T(128)}, u32[]{:S(2)}) %copy-start) | copy-done | bytes 32
  1.8 0.0 copy-start.1
  1.8 0.7 %copy-done.1 = s32[16]{0:T(128)S(1)} copy-done((s32[16]{0:T(128)S(1)}, s32[16]{0:T(128)}, u32[]{:S(2)}) %copy-start.1) | copy-done | bytes 88
  2.4 49.1 %shard_map.46 = bf16[32,2048]{1,0:T(8,128)(2,1)S(1)} custom-call(s32[2]{0:T(128)S(1)} %copy-done, s32[16]{0:T(128)S(1)} %copy-done.1, bf16[2,128,1152]{2,1,0:T(8,128)(2,1)S(1)} %bitcast.5, bf16[2560,1024]{1,0:T(8,128)(2,1)} %constant.2.clone.tables_hbm), custom_call_target="tpu_custom_call" | custom-call | flops 3000000000 | bytes 7000000 | tf_op jit(solution)/shard_map/pallas_call | solution.py:582
  51.6 0.7 %copy.6 = bf16[4,8,16,128]{3,2,1,0:T(8,128)(2,1)} copy(bf16[4,8,16,128]{3,1,2,0:T(8,128)(2,1)S(1)} %bitcast.6) | data formatting | bytes 262144
Async XLA Ops:
  1.1 0.7 %copy-start = (s32[2]{0:T(128)S(1)}, s32[2]{0:T(128)}, u32[]{:S(2)}) copy-start(s32[2]{0:T(128)} %offsets_hbm.1) | copy-start | bytes 28
  1.8 0.7 %copy-start.1 = (s32[16]{0:T(128)S(1)}, s32[16]{0:T(128)}, u32[]{:S(2)}) copy-start(s32[16]{0:T(128)} %sources_hbm.1) | copy-start | bytes 196

commit v6 on v5

--- a/solution.py
+++ b/solution.py
@@ -19,11 +19,13 @@
 WIN = 2
 BLK = ROWS // NX
 GROUPS = 32
+SKIP = 40
 NLOW = 2
 NZ = 4
 CHUNKS = 2
 PART = BLK // CHUNKS
 WIDE = NSRC * PART
+BINS = np.concatenate([np.arange(0, HALF, 2), np.arange(1, HALF, 2)])
 F32 = jnp.float32
 BF16 = jnp.bfloat16
 MESH = pl.DeviceIdType.MESH
@@ -32,7 +34,7 @@
 def forward_tables():
     rows = np.arange(SAMPLES)[:, None]
     cols = np.arange(SAMPLES)[None, :]
-    freq = rows % HALF
+    freq = BINS[rows % HALF]
     angle = 2.0 * np.pi / SAMPLES * (freq * cols % SAMPLES)
     alternating = 1.0 - 2.0 * (cols % 2)
     imag = np.where(freq == 0, alternating, -np.sin(angle))
@@ -44,7 +46,7 @@
 
 def inverse_table(windows):
     shifted = np.arange(HALF)[:, None] - HALF // 2
-    freq = (np.arange(16)[:, None] + 16 * np.arange(GROUPS)[None, :]).reshape(1, -1)
+    freq = BINS[(np.arange(16)[:, None] + 16 * np.arange(GROUPS)[None, :]).reshape(1, -1)]
     angle = 2.0 * np.pi / SAMPLES * (freq * shifted % SAMPLES)
     alternating = 1.0 - 2.0 * (shifted % 2)
     first = freq == 0
@@ -92,6 +94,8 @@
     sources,
     upper,
     lower,
+    upper_t,
+    lower_t,
     inverse,
     traces,
     pieces,
@@ -177,7 +181,9 @@
                 (sources_hbm, sources),
                 (tables_hbm.at[pl.ds(0, SAMPLES)], upper),
                 (tables_hbm.at[pl.ds(SAMPLES, SAMPLES)], lower),
-                (tables_hbm.at[pl.ds(2 * SAMPLES, HALF)], inverse),
+                (tables_hbm.at[pl.ds(2 * SAMPLES, HALF)], upper_t),
+                (tables_hbm.at[pl.ds(2 * SAMPLES + HALF, HALF)], lower_t),
+                (tables_hbm.at[pl.ds(3 * SAMPLES, HALF)], inverse),
             ]
         )
     ]
@@ -346,13 +352,24 @@
     def _(step):
         y_copy(me_y, lax.rem(me_y + step, ny)).wait_recv()
 
+    loads[4].wait()
+    loads[5].wait()
     total = parts_y[0].astype(F32)
     for i in range(1, ny):
         total = total + parts_y[i].astype(F32)
-    rows = jnp.concatenate([total[:8], total[8:]], axis=1).astype(BF16)
-    both = dot_t(rows, upper[...]) + dot_t(rows, lower[...])
-    re = both[:, :HALF]
-    im = both[:, HALF:]
+    folded = []
+    for rows in (total[:8] + total[8:], total[:8] - total[8:]):
+        high = rows.astype(BF16)
+        rest = (rows - high.astype(F32)).astype(BF16)
+        folded.append(jnp.concatenate([high, rest], axis=0))
+
+    def quarter(i):
+        at = pl.ds(i * HALF // 2, HALF // 2)
+        both = dot(folded[i % 2], upper_t[:, at]) + dot(folded[i % 2], lower_t[:, at])
+        return both[:8] + both[8:]
+
+    re = jnp.concatenate([quarter(0), quarter(1)], axis=1)
+    im = jnp.concatenate([quarter(2), quarter(3)], axis=1)
     size = jnp.sqrt(re * re + im * im)
     first = lax.broadcasted_iota(jnp.int32, (8, HALF), 1) == 0
     total = jnp.sum(
@@ -440,11 +457,11 @@
                 )
                 result = dot(rows_left, right[chunk, group])
                 for h in range(2):
-                    cross[chunk, h, pl.ds(group, 32, stride=32), :] = result[
+                    cross[chunk, h, pl.ds(group, 32, stride=SKIP), :] = result[
                         :, 128 * h : 128 * h + 128
                     ]
 
-    loads[4].wait()
+    loads[6].wait()
 
     ahead = lax.rem(me_z + 1, NZ)
     behind = lax.rem(me_z + NZ - 1, NZ)
@@ -477,7 +494,7 @@
             for octet in range(2):
                 for h in range(2):
                     parts = [
-                        cross[chunk, h, pl.ds((part * 16 + octet * 8 + i) * 32, 32), :].astype(BF16)
+                        cross[chunk, h, pl.ds((part * 16 + octet * 8 + i) * SKIP, 32), :].astype(BF16)
                         for i in range(8)
                     ]
                     parts = block_transpose(parts)
@@ -575,7 +592,7 @@
     own = lag_rows // NX
     upper, lower = forward_tables()
     inverse = inverse_table(NZ * NX * WIN)
-    tables = np.concatenate([upper, lower, inverse], axis=0)
+    tables = np.concatenate([upper, lower, upper.T[:HALF], lower.T[:HALF], inverse], axis=0)
     vmem = pl.BlockSpec(memory_space=pltpu.VMEM)
     hbm = pl.BlockSpec(memory_space=pltpu.HBM)
     dma = pltpu.SemaphoreType.DMA
@@ -590,6 +607,8 @@
             pltpu.VMEM((SAMPLES, SAMPLES), BF16),
             pltpu.VMEM((SAMPLES, SAMPLES), BF16),
             pltpu.VMEM((HALF, SAMPLES), BF16),
+            pltpu.VMEM((HALF, SAMPLES), BF16),
+            pltpu.VMEM((HALF, SAMPLES), BF16),
             pltpu.VMEM((256, SAMPLES), BF16),
             pltpu.VMEM((2 * NLOW, 16, HALF), BF16),
             pltpu.VMEM((2 * NLOW, 16, HALF), BF16),
@@ -601,7 +620,7 @@
             pltpu.VMEM((8, 2, 2, 64, 128), BF16),
             pltpu.VMEM((HALF, 1024), BF16),
             pltpu.VMEM((CHUNKS, GROUPS, 256, 256), BF16),
-            pltpu.VMEM((CHUNKS, 2, SAMPLES, 128), F32),
+            pltpu.VMEM((CHUNKS, 2, 32 * SKIP, 128), F32),
             pltpu.VMEM((SAMPLES, 512), BF16),
             pltpu.VMEM((CHUNKS, 3, lag_rows, WIDE), BF16),
             pltpu.VMEM((CHUNKS, 2, lag_rows // 2, WIDE), BF16),
@@ -609,7 +628,7 @@
             pltpu.VMEM((CHUNKS, 3, 2, lag_rows // 2, WIDE), BF16),
             pltpu.VMEM((CHUNKS, lag_rows, WIDE), BF16),
             pltpu.VMEM((CHUNKS, NX, own, WIDE), BF16),
-            dma((5,)),
+            dma((7,)),
             dma((2 * NLOW,)),
             dma((2 * NLOW,)),
             dma((ny,)),

time: 52.4 us -> 52.7 us (level)
  the two profiles are of different devices: /device:TPU:1 before, /device:TPU:8 now
where the time goes in v6:
time: 52.7 us; the launch traced here: 52.5 us
  Pallas kernels  49.4 us (94%)
  local copies, waits for them, and re-layouts  3.11 us (6%)
    pallas_call x1, Pallas kernels, local(): pl.pallas_call(functools.partial(kernel, ny), out_shape=jax.ShapeDtypeStr...  49.4 us
    unnamed x6, local copies, waits for them, and re-layouts  3.11 us

profile of v6, /device:TPU:8, one launch (start us, length us, event | category | flops | bytes accessed | tf_op | source)
XLA Modules:
  0.0 52.5 jit_solution(10361027041199381220)
XLA Ops:
  0.0 1.1 %copy.8 = bf16[128,2,1152]{2,0,1:T(8,128)(2,1)S(1)} copy(bf16[128,2,1152]{2,1,0:T(2,128)(2,1)} %param.4) | data formatting | bytes 1179648 | tf_op args[0]
  1.1 0.0 copy-start
  1.1 0.6 %copy-done = s32[2]{0:T(128)S(1)} copy-done((s32[2]{0:T(128)S(1)}, s32[2]{0:T(128)}, u32[]{:S(2)}) %copy-start) | copy-done | bytes 32
  1.8 0.0 copy-start.1
  1.8 0.7 %copy-done.1 = s32[16]{0:T(128)S(1)} copy-done((s32[16]{0:T(128)S(1)}, s32[16]{0:T(128)}, u32[]{:S(2)}) %copy-start.1) | copy-done | bytes 88
  2.4 49.4 %shard_map.46 = bf16[32,2048]{1,0:T(8,128)(2,1)S(1)} custom-call(s32[2]{0:T(128)S(1)} %copy-done, s32[16]{0:T(128)S(1)} %copy-done.1, bf16[2,128,1152]{2,1,0:T(8,128)(2,1)S(1)} %bitcast.5, bf16[3584,1024]{1,0:T(8,128)(2,1)} %constant.2.clone.tables_hbm), custom_call_target="tpu_custom_call" | custom-call | flops 3000000000 | bytes 7000000 | tf_op jit(solution)/shard_map/pallas_call | solution.py:599
  51.8 0.7 %copy.6 = bf16[4,8,16,128]{3,2,1,0:T(8,128)(2,1)} copy(bf16[4,8,16,128]{3,1,2,0:T(8,128)(2,1)S(1)} %bitcast.6) | data formatting | bytes 262144
Async XLA Ops:
  1.1 0.7 %copy-start = (s32[2]{0:T(128)S(1)}, s32[2]{0:T(128)}, u32[]{:S(2)}) copy-start(s32[2]{0:T(128)} %offsets_hbm.1) | copy-start | bytes 28
  1.8 0.7 %copy-start.1 = (s32[16]{0:T(128)S(1)}, s32[16]{0:T(128)}, u32[]{:S(2)}) copy-start(s32[16]{0:T(128)} %sources_hbm.1) | copy-start | bytes 196

commit v7 on v6

--- a/solution.py
+++ b/solution.py
@@ -251,26 +251,6 @@
     loads[2].wait()
     spectrum[...] = dot_t(upper[...], traces[...])
 
-    for step in (1, 2, 3):
-        near_copy(me_near, lax.rem(me_near + step, near)).wait_recv()
-    total = reduced[0].astype(F32)
-    for i in range(1, near):
-        total = total + reduced[i].astype(F32)
-    parts_y[me_y] = total.astype(BF16)
-
-    def y_copy(to, slot):
-        return pltpu.make_async_remote_copy(
-            src_ref=parts_y.at[me_y],
-            dst_ref=parts_y.at[slot],
-            send_sem=y_send.at[to],
-            recv_sem=y_recv.at[slot],
-            device_id=at_y(to),
-            device_id_type=MESH,
-        )
-
-    for step in sorted(range(1, ny), key=lambda step: -min(step, ny - step)):
-        y_copy(lax.rem(me_y + step, ny), me_y).start()
-
     loads[3].wait()
     spectrum[...] += dot_t(lower[...], traces[...])
 
@@ -317,6 +297,26 @@
 
     for step in (2, 1, 3):
         white_copy(lax.rem(me_x + step, NX), me_x).start()
+    for step in (1, 2, 3):
+        near_copy(me_near, lax.rem(me_near + step, near)).wait_recv()
+    total = reduced[0].astype(F32)
+    for i in range(1, near):
+        total = total + reduced[i].astype(F32)
+    parts_y[me_y] = total.astype(BF16)
+
+    def y_copy(to, slot):
+        return pltpu.make_async_remote_copy(
+            src_ref=parts_y.at[me_y],
+            dst_ref=parts_y.at[slot],
+            send_sem=y_send.at[to],
+            recv_sem=y_recv.at[slot],
+            device_id=at_y(to),
+            device_id_type=MESH,
+        )
+
+    for step in sorted(range(1, ny), key=lambda step: -min(step, ny - step)):
+        y_copy(lax.rem(me_y + step, ny), me_y).start()
+
     incoming[me_x] = outgoing[me_x]
 
     r = lax.broadcasted_iota(jnp.int32, (128, 1024), 0)

time: 52.7 us -> 49.6 us (0.941)
  the two profiles are of different devices: /device:TPU:8 before, /device:TPU:1 now
where the time goes in v7:
time: 49.6 us; the launch traced here: 49.3 us
  Pallas kernels  46.2 us (93%)
  local copies, waits for them, and re-layouts  3.11 us (6%)
    pallas_call x1, Pallas kernels, local(): pl.pallas_call(functools.partial(kernel, ny), out_shape=jax.ShapeDtypeStr...  46.2 us
    unnamed x6, local copies, waits for them, and re-layouts  3.11 us

profile of v7, /device:TPU:1, one launch (start us, length us, event | category | flops | bytes accessed | tf_op | source)
XLA Modules:
  0.0 49.3 jit_solution(13918052175585167254)
XLA Ops:
  0.0 1.1 %copy.8 = bf16[128,2,1152]{2,0,1:T(8,128)(2,1)S(1)} copy(bf16[128,2,1152]{2,1,0:T(2,128)(2,1)} %param.4) | data formatting | bytes 1179648 | tf_op args[0]
  1.1 0.0 copy-start
  1.1 0.6 %copy-done = s32[2]{0:T(128)S(1)} copy-done((s32[2]{0:T(128)S(1)}, s32[2]{0:T(128)}, u32[]{:S(2)}) %copy-start) | copy-done | bytes 32
  1.8 0.0 copy-start.1
  1.8 0.7 %copy-done.1 = s32[16]{0:T(128)S(1)} copy-done((s32[16]{0:T(128)S(1)}, s32[16]{0:T(128)}, u32[]{:S(2)}) %copy-start.1) | copy-done | bytes 88
  2.4 46.2 %shard_map.46 = bf16[32,2048]{1,0:T(8,128)(2,1)S(1)} custom-call(s32[2]{0:T(128)S(1)} %copy-done, s32[16]{0:T(128)S(1)} %copy-done.1, bf16[2,128,1152]{2,1,0:T(8,128)(2,1)S(1)} %bitcast.5, bf16[3584,1024]{1,0:T(8,128)(2,1)} %constant.2.clone.tables_hbm), custom_call_target="tpu_custom_call" | custom-call | flops 3000000000 | bytes 7000000 | tf_op jit(solution)/shard_map/pallas_call | solution.py:599
  48.6 0.7 %copy.6 = bf16[4,8,16,128]{3,2,1,0:T(8,128)(2,1)} copy(bf16[4,8,16,128]{3,1,2,0:T(8,128)(2,1)S(1)} %bitcast.6) | data formatting | bytes 262144
Async XLA Ops:
  1.1 0.7 %copy-start = (s32[2]{0:T(128)S(1)}, s32[2]{0:T(128)}, u32[]{:S(2)}) copy-start(s32[2]{0:T(128)} %offsets_hbm.1) | copy-start | bytes 28
  1.8 0.7 %copy-start.1 = (s32[16]{0:T(128)S(1)}, s32[16]{0:T(128)}, u32[]{:S(2)}) copy-start(s32[16]{0:T(128)} %sources_hbm.1) | copy-start | bytes 196

commit v8 on v7

--- a/solution.py
+++ b/solution.py
@@ -187,7 +187,7 @@
             ]
         )
     ]
-    for load in loads:
+    for load in loads[:3]:
         load.start()
 
     barrier = pltpu.get_barrier_semaphore()
@@ -207,6 +207,7 @@
 
     loads[0].wait()
     loads[1].wait()
+    loads[3].start()
 
     lane = lax.broadcasted_iota(jnp.int32, (ROWS, 128), 1)
     for w in range(WIN):
@@ -249,6 +250,8 @@
         near_copy(lax.rem(me_near + step, near), me_near).start()
     reduced[me_near] = pieces[me_near]
     loads[2].wait()
+    for load in loads[4:]:
+        load.start()
     spectrum[...] = dot_t(upper[...], traces[...])
 
     loads[3].wait()
@@ -419,11 +422,11 @@
                         tiles.append(
                             half[8 * part : 8 * part + 8, 128 * big : 128 * big + 128]
                         )
-            parts.append(jnp.concatenate(tiles, axis=0))
+            parts.append(jnp.concatenate(tiles, axis=0).astype(BF16))
     parts = block_transpose(parts)
     for small in range(8):
-        a_re = parts[small][:64].astype(BF16)
-        a_im = parts[small][64:].astype(BF16)
+        a_re = parts[small][:64]
+        a_im = parts[small][64:]
         re_b0, re_b1, im_b0, im_b1 = a_re, a_im, -a_im, a_re
         if small == 0:
             shape = (64, 128)

time: 49.6 us -> 49.5 us (level)
  no operation moved by 1% of the time
where the time goes in v8:
time: 49.5 us; the launch traced here: 49.2 us
  Pallas kernels  46 us (93%)
  local copies, waits for them, and re-layouts  3.11 us (6%)
    pallas_call x1, Pallas kernels, local(): pl.pallas_call(functools.partial(kernel, ny), out_shape=jax.ShapeDtypeStr...  46 us
    unnamed x6, local copies, waits for them, and re-layouts  3.11 us

profile of v8, /device:TPU:1, one launch (start us, length us, event | category | flops | bytes accessed | tf_op | source)
XLA Modules:
  0.0 49.2 jit_solution(13492562124047280998)
XLA Ops:
  0.0 1.1 %copy.8 = bf16[128,2,1152]{2,0,1:T(8,128)(2,1)S(1)} copy(bf16[128,2,1152]{2,1,0:T(2,128)(2,1)} %param.4) | data formatting | bytes 1179648 | tf_op args[0]
  1.1 0.0 copy-start
  1.1 0.6 %copy-done = s32[2]{0:T(128)S(1)} copy-done((s32[2]{0:T(128)S(1)}, s32[2]{0:T(128)}, u32[]{:S(2)}) %copy-start) | copy-done | bytes 32
  1.8 0.0 copy-start.1
  1.8 0.7 %copy-done.1 = s32[16]{0:T(128)S(1)} copy-done((s32[16]{0:T(128)S(1)}, s32[16]{0:T(128)}, u32[]{:S(2)}) %copy-start.1) | copy-done | bytes 88
  2.4 46.0 %shard_map.46 = bf16[32,2048]{1,0:T(8,128)(2,1)S(1)} custom-call(s32[2]{0:T(128)S(1)} %copy-done, s32[16]{0:T(128)S(1)} %copy-done.1, bf16[2,128,1152]{2,1,0:T(8,128)(2,1)S(1)} %bitcast.5, bf16[3584,1024]{1,0:T(8,128)(2,1)} %constant.2.clone.tables_hbm), custom_call_target="tpu_custom_call" | custom-call | flops 3000000000 | bytes 7000000 | tf_op jit(solution)/shard_map/pallas_call | solution.py:602
  48.5 0.7 %copy.6 = bf16[4,8,16,128]{3,2,1,0:T(8,128)(2,1)} copy(bf16[4,8,16,128]{3,1,2,0:T(8,128)(2,1)S(1)} %bitcast.6) | data formatting | bytes 262144
Async XLA Ops:
  1.1 0.7 %copy-start = (s32[2]{0:T(128)S(1)}, s32[2]{0:T(128)}, u32[]{:S(2)}) copy-start(s32[2]{0:T(128)} %offsets_hbm.1) | copy-start | bytes 28
  1.8 0.7 %copy-start.1 = (s32[16]{0:T(128)S(1)}, s32[16]{0:T(128)}, u32[]{:S(2)}) copy-start(s32[16]{0:T(128)} %sources_hbm.1) | copy-start | bytes 196

commit v9 on v8

--- a/solution.py
+++ b/solution.py
@@ -623,7 +623,7 @@
             pltpu.VMEM((8, 2, 2, 64, 128), BF16),
             pltpu.VMEM((HALF, 1024), BF16),
             pltpu.VMEM((CHUNKS, GROUPS, 256, 256), BF16),
-            pltpu.VMEM((CHUNKS, 2, 32 * SKIP, 128), F32),
+            pltpu.VMEM((CHUNKS, 2, 33 * SKIP, 128), F32),
             pltpu.VMEM((SAMPLES, 512), BF16),
             pltpu.VMEM((CHUNKS, 3, lag_rows, WIDE), BF16),
             pltpu.VMEM((CHUNKS, 2, lag_rows // 2, WIDE), BF16),

time: 49.5 us -> 49.5 us (level)
  no operation moved by 1% of the time
where the time goes in v9:
time: 49.5 us; the launch traced here: 49.2 us
  Pallas kernels  46 us (93%)
  local copies, waits for them, and re-layouts  3.11 us (6%)
    pallas_call x1, Pallas kernels, local(): pl.pallas_call(functools.partial(kernel, ny), out_shape=jax.ShapeDtypeStr...  46 us
    unnamed x6, local copies, waits for them, and re-layouts  3.11 us

profile of v9, /device:TPU:1, one launch (start us, length us, event | category | flops | bytes accessed | tf_op | source)
XLA Modules:
  0.0 49.2 jit_solution(10635543717061843269)
XLA Ops:
  0.0 1.1 %copy.8 = bf16[128,2,1152]{2,0,1:T(8,128)(2,1)S(1)} copy(bf16[128,2,1152]{2,1,0:T(2,128)(2,1)} %param.4) | data formatting | bytes 1179648 | tf_op args[0]
  1.1 0.0 copy-start
  1.1 0.6 %copy-done = s32[2]{0:T(128)S(1)} copy-done((s32[2]{0:T(128)S(1)}, s32[2]{0:T(128)}, u32[]{:S(2)}) %copy-start) | copy-done | bytes 32
  1.8 0.0 copy-start.1
  1.8 0.7 %copy-done.1 = s32[16]{0:T(128)S(1)} copy-done((s32[16]{0:T(128)S(1)}, s32[16]{0:T(128)}, u32[]{:S(2)}) %copy-start.1) | copy-done | bytes 88
  2.4 46.0 %shard_map.46 = bf16[32,2048]{1,0:T(8,128)(2,1)S(1)} custom-call(s32[2]{0:T(128)S(1)} %copy-done, s32[16]{0:T(128)S(1)} %copy-done.1, bf16[2,128,1152]{2,1,0:T(8,128)(2,1)S(1)} %bitcast.5, bf16[3584,1024]{1,0:T(8,128)(2,1)} %constant.2.clone.tables_hbm), custom_call_target="tpu_custom_call" | custom-call | flops 3000000000 | bytes 7000000 | tf_op jit(solution)/shard_map/pallas_call | solution.py:602
  48.5 0.7 %copy.6 = bf16[4,8,16,128]{3,2,1,0:T(8,128)(2,1)} copy(bf16[4,8,16,128]{3,1,2,0:T(8,128)(2,1)S(1)} %bitcast.6) | data formatting | bytes 262144
Async XLA Ops:
  1.1 0.7 %copy-start = (s32[2]{0:T(128)S(1)}, s32[2]{0:T(128)}, u32[]{:S(2)}) copy-start(s32[2]{0:T(128)} %offsets_hbm.1) | copy-start | bytes 28
  1.8 0.7 %copy-start.1 = (s32[16]{0:T(128)S(1)}, s32[16]{0:T(128)}, u32[]{:S(2)}) copy-start(s32[16]{0:T(128)} %sources_hbm.1) | copy-start | bytes 196
